TPU v7x, 128 devices: a whole 4x4x4 slice. The times are simulated.
128 devices in a mesh: dp: 4 (over x), outer: 16 (over z, y), inner: 2 (over core).
Axes of the slice: x: 4, y: 4, z: 4, core: 2. Of those that a mesh axis runs over, the one named last changes fastest.
Arguments:
- queries: bfloat16 [4, 4096, 1024], P('dp', ('outer', 'inner')), may hold values from -6 to 6
- keys: bfloat16 [4, 4096, 2, 1024], P('dp', ('outer', 'inner')), may hold values from -6 to 6
- values: bfloat16 [4, 4096, 2, 1024], P('dp', ('outer', 'inner')), may hold values from -6 to 6
- betas: float32 [4, 8, 2, 4096], P('dp', None, None, ('outer', 'inner')), may hold values from 0.3 to 1.6
- grad_out: bfloat16 [4, 4096, 1024], P('dp', ('outer', 'inner')), may hold values from -16 to 16
- gain: float32 [1024], replicated, may hold values from 0.1 to 1.9
Outputs:
- grad_queries: bfloat16 [4, 4096, 1024], P('dp', ('outer', 'inner'))
- grad_keys: bfloat16 [4, 4096, 2, 1024], P('dp', ('outer', 'inner'))
- grad_values: bfloat16 [4, 4096, 2, 1024], P('dp', ('outer', 'inner'))
- gain_grad: float32 [1024], replicated
All inputs are finite; a program needn't handle non-finite values.
Results may differ from a plain program's by a relative error of at most 0.001.
Values sent between devices are 32-bit elements; how exact they have to be, the bound alone decides.
A program may use at most 128 MiB of HBM per device.

v0:
```python
import math

import jax
import jax.numpy as jnp
from jax import lax
from jax.sharding import PartitionSpec as P

HEADS = 8
HEAD_DIM = 128
STRETCH = 64


EXACT = lax.Precision.HIGHEST
EPS_KEY = 1e-06
EPS_OUT = 1e-05


def passed_along(block, axis, distance):
    devices = range(lax.axis_size(axis))
    route = [(i - distance, i) for i in devices if i - distance in devices]
    return lax.ppermute(block, axis, route)


def spread(value, axis, source):
    kept = jnp.where(lax.axis_index(axis) == source, value, 0).astype(value.dtype)
    return lax.psum(kept, axis)


def prefix(shard, axis, combine, identity, reverse):
    size, here = (lax.axis_size(axis), lax.axis_index(axis))
    everything = lax.all_gather(shard, axis)
    start = jnp.broadcast_to(jnp.asarray(identity, shard.dtype), shard.shape)

    def step(k, before):
        at = size - 1 - k if reverse else k
        reached = at > here if reverse else at < here
        new = combine(before, everything[at])
        return jnp.where(reached, new, before)

    return lax.fori_loop(0, size, step, start)


def product(spec, left, right):
    return jnp.einsum(spec, left, right, precision=EXACT, preferred_element_type=jnp.float32)


def unit_rows(raw):
    scale_inv = lax.rsqrt(jnp.sum(raw * raw, axis=-1, keepdims=True) + EPS_KEY)
    return (raw * scale_inv, scale_inv)


def unit_back(unit, scale_inv, grad):
    return scale_inv * (grad - unit * jnp.sum(unit * grad, axis=-1, keepdims=True))


def compose(earlier, later):
    through = product("mhij,hjk->mhik", earlier, later[0])
    return through + jnp.stack([jnp.zeros_like(later[1]), later[1]])


def stretch_factors(key_blk, value_blk, rate_blk, strict, eye_refl, eye_head):
    head_dim = key_blk.shape[2]
    gram = product("hrd,hsd->hrs", key_blk, key_blk)
    lower_mat = eye_refl + rate_blk[:, :, None] * gram * strict
    rhs = jnp.concatenate(
        [rate_blk[:, :, None] * key_blk, rate_blk[:, :, None] * value_blk], axis=2
    )
    solved = jax.scipy.linalg.solve_triangular(lower_mat, rhs, lower=True)
    w_mat = solved[:, :, :head_dim]
    t_vals = solved[:, :, head_dim:]
    transit = eye_head - product("hrd,hre->hde", w_mat, key_blk)
    return (lower_mat, w_mat, t_vals, transit)


def forward_nested(own_map, identity):
    count = lax.axis_size("inner")
    first = lax.axis_index("inner") == 0
    acc_map = identity
    sent = compose(acc_map, own_map)
    got = passed_along(sent, "inner", 1)
    acc_map = jnp.stack([jnp.where(first, identity[0], got[0]), got[1]])
    group_map = spread(compose(acc_map, own_map), "inner", count - 1)
    before = prefix(group_map, "outer", compose, identity, False)
    return compose(before, acc_map)


def backward_nested(own_map, identity):
    count = lax.axis_size("inner")
    final = lax.axis_index("inner") == count - 1
    acc_map = identity
    sent = compose(acc_map, own_map)
    got = passed_along(sent, "inner", -1)
    acc_map = jnp.stack([jnp.where(final, identity[0], got[0]), got[1]])
    group_map = spread(compose(acc_map, own_map), "inner", 0)
    after = prefix(group_map, "outer", compose, identity, True)
    return compose(after, acc_map)


def on_device(queries, keys, values, betas, grad_out, gain):
    length_here = queries.shape[1]
    heads = HEADS
    head_dim = HEAD_DIM
    span = STRETCH
    refl = 2 * span
    count = length_here // span
    query_raw = (
        queries[0].astype(jnp.float32).reshape(length_here, heads, head_dim).transpose(1, 0, 2)
    )
    key_raw = (
        keys[0]
        .astype(jnp.float32)
        .reshape(length_here, 2, heads, head_dim)
        .transpose(2, 0, 1, 3)
        .reshape(heads, 2 * length_here, head_dim)
    )
    value_all = (
        values[0]
        .astype(jnp.float32)
        .reshape(length_here, 2, heads, head_dim)
        .transpose(2, 0, 1, 3)
        .reshape(heads, 2 * length_here, head_dim)
    )
    rate_all = betas[0].transpose(0, 2, 1).reshape(heads, 2 * length_here)
    cotan_all = (
        grad_out[0].astype(jnp.float32).reshape(length_here, heads, head_dim).transpose(1, 0, 2)
    )
    gains = gain.reshape(heads, head_dim)
    query_n, query_inv = unit_rows(query_raw)
    key_n, key_inv = unit_rows(key_raw)
    token_ids = lax.broadcasted_iota(jnp.int32, (span, refl), 0)
    refl_ids = lax.broadcasted_iota(jnp.int32, (span, refl), 1)
    read_mask = (refl_ids <= 2 * token_ids + 1).astype(jnp.float32)
    row_ids = lax.broadcasted_iota(jnp.int32, (refl, refl), 0)
    col_ids = lax.broadcasted_iota(jnp.int32, (refl, refl), 1)
    strict = (col_ids < row_ids).astype(jnp.float32)
    eye_refl = jnp.eye(refl, dtype=jnp.float32)
    eye_head = jnp.eye(head_dim, dtype=jnp.float32)
    identity = jnp.stack(
        [
            jnp.broadcast_to(eye_head, (heads, head_dim, head_dim)),
            jnp.zeros((heads, head_dim, head_dim), jnp.float32),
        ]
    )

    def refl_rows(array, block_id):
        return array[:, block_id * refl : (block_id + 1) * refl]

    def token_rows(array, block_id):
        return array[:, block_id * span : (block_id + 1) * span]

    stash = []
    block_map = identity
    for block_id in range(count):
        key_blk = refl_rows(key_n, block_id)
        factor_set = stretch_factors(
            key_blk,
            refl_rows(value_all, block_id),
            refl_rows(rate_all, block_id),
            strict,
            eye_refl,
            eye_head,
        )
        offset = product("hrv,hre->hve", factor_set[2], key_blk)
        block_map = compose(block_map, jnp.stack([factor_set[3], offset]))
        stash.append(factor_set)

    def factors_of(block_id):
        return stash[block_id]

    state = forward_nested(block_map, identity)[1]
    records = []
    adjoint_maps = []
    gain_sum = jnp.zeros((heads, head_dim), jnp.float32)
    for block_id in range(count):
        lower_mat, w_mat, t_vals, transit = factors_of(block_id)
        key_blk = refl_rows(key_n, block_id)
        query_blk = token_rows(query_n, block_id)
        cotan_blk = token_rows(cotan_all, block_id)
        update = t_vals - product("hrk,hvk->hrv", w_mat, state)
        scores = product("htd,hrd->htr", query_blk, key_blk) * read_mask
        output = product("htk,hvk->htv", query_blk, state) + product("htr,hrv->htv", scores, update)
        scale_inv = lax.rsqrt(jnp.mean(output * output, axis=2, keepdims=True) + EPS_OUT)
        normed = output * scale_inv
        scaled = cotan_blk * gains[:, None, :]
        d_out = scale_inv * (scaled - normed * jnp.mean(normed * scaled, axis=2, keepdims=True))
        gain_sum = gain_sum + jnp.sum(cotan_blk * normed, axis=1)
        source = product("htv,htk->hvk", d_out, query_blk - product("htr,hrk->htk", scores, w_mat))
        records.append((state, update, scores, d_out))
        adjoint_maps.append(jnp.stack([jnp.swapaxes(transit, 1, 2), source]))
        state = state + product("hrv,hrk->hvk", update, key_blk)
    adjoint_block = identity
    for block_id in reversed(range(count)):
        adjoint_block = compose(adjoint_block, adjoint_maps[block_id])
    adjoint = backward_nested(adjoint_block, identity)[1]
    grad_q_parts = [None] * count
    grad_k_parts = [None] * count
    grad_v_parts = [None] * count
    for block_id in reversed(range(count)):
        lower_mat, w_mat, t_vals, transit = factors_of(block_id)
        start_state, update, scores, d_out = records[block_id]
        key_blk = refl_rows(key_n, block_id)
        query_blk = token_rows(query_n, block_id)
        rate_blk = refl_rows(rate_all, block_id)
        d_update = product("htr,htv->hrv", scores, d_out) + product(
            "hrk,hvk->hrv", key_blk, adjoint
        )
        solved = jax.scipy.linalg.solve_triangular(lower_mat, d_update, trans=1, lower=True)
        d_target = rate_blk[:, :, None] * solved
        d_scores = product("htv,hrv->htr", d_out, update) * read_mask
        grad_q_parts[block_id] = product("htv,hvk->htk", d_out, start_state) + product(
            "htr,hrk->htk", d_scores, key_blk
        )
        d_gram = -product("hrv,hsv->hrs", d_target, update) * strict
        grad_k_parts[block_id] = (
            product("hrv,hvk->hrk", update, adjoint)
            + product("htr,htk->hrk", d_scores, query_blk)
            - product("hrv,hvk->hrk", d_target, start_state)
            + product("hrs,hsk->hrk", d_gram + jnp.swapaxes(d_gram, 1, 2), key_blk)
        )
        grad_v_parts[block_id] = d_target
        adjoint = (
            adjoint
            + product("htv,htk->hvk", d_out, query_blk)
            - product("hrv,hrk->hvk", d_target, key_blk)
        )
    grad_qn = jnp.concatenate(grad_q_parts, axis=1)
    grad_kn = jnp.concatenate(grad_k_parts, axis=1)
    grad_val = jnp.concatenate(grad_v_parts, axis=1)
    grad_q = unit_back(query_n, query_inv, grad_qn)
    grad_k = unit_back(key_n, key_inv, grad_kn)
    grad_q = (
        grad_q.transpose(1, 0, 2).reshape(1, length_here, heads * head_dim).astype(jnp.bfloat16)
    )
    grad_k = (
        grad_k.reshape(heads, length_here, 2, head_dim)
        .transpose(1, 2, 0, 3)
        .reshape(1, length_here, 2, heads * head_dim)
        .astype(jnp.bfloat16)
    )
    grad_val = (
        grad_val.reshape(heads, length_here, 2, head_dim)
        .transpose(1, 2, 0, 3)
        .reshape(1, length_here, 2, heads * head_dim)
        .astype(jnp.bfloat16)
    )
    total = lax.psum(gain_sum, ("dp", "outer", "inner"))
    tokens_all = length_here * lax.axis_size("dp") * lax.axis_size("outer") * lax.axis_size("inner")
    gain_grad = total.reshape(heads * head_dim) * (1.0 / math.sqrt(tokens_all))
    return (grad_q, grad_k, grad_val, gain_grad)


def solution(mesh):
    return jax.shard_map(
        on_device,
        mesh=mesh,
        in_specs=(
            P("dp", ("outer", "inner"), None),
            P("dp", ("outer", "inner"), None, None),
            P("dp", ("outer", "inner"), None, None),
            P("dp", None, None, ("outer", "inner")),
            P("dp", ("outer", "inner"), None),
            P(),
        ),
        out_specs=(
            P("dp", ("outer", "inner"), None),
            P("dp", ("outer", "inner"), None, None),
            P("dp", ("outer", "inner"), None, None),
            P(),
        ),
        check_vma=False,
    )
```

profile of v0, /device:TPU:1, one launch (start us, length us, event | category | flops | bytes accessed | tf_op | source)
XLA Modules:
  0.0 764.0 jit_solution(11340195129437190525)
XLA Ops:
  13.8 79.8 %custom-call.9 = f32[8,1,128,128]{2,3,1,0:T(8,128)} custom-call(f32[8,1,128,128]{3,2,1,0:T(8,128)S(1)} %fusion.54), custom_call_target="InvertDiagBlocksLowerTriangular" | custom-call | tf_op jit(solution)/shard_map/jit(_solve_triangular)/vmap()/triangular_solve | solution.py:68
  103.9 79.4 %custom-call.8 = f32[8,1,128,128]{2,3,1,0:T(8,128)} custom-call(f32[8,1,128,128]{3,2,1,0:T(8,128)S(1)} %fusion.59), custom_call_target="InvertDiagBlocksLowerTriangular" | custom-call | tf_op jit(solution)/shard_map/jit(_solve_triangular)/vmap()/triangular_solve | solution.py:68
  196.4 3.9 collective-permute-done
  201.6 3.4 fusion.47
  205.1 28.1 %all-reduce.14.cloned.1.call-done = f32[1,2,8,128,128]{4,3,2,1,0:T(8,128)} async-done(((f32[1,2,8,128,128]{4,3,2,1,0:T(8,128)}), f32[1,2,8,128,128]{4,3,2,1,0:T(8,128)}) %all-reduce.14.cloned.1.call-update) | async-done | bytes 1048592 | tf_op jit(solution)/shard_map/psum | solution.py:26
  247.2 100.7 %all-gather.3.cloned.1.call-done = f32[16,2,8,128,128]{4,3,2,1,0:T(8,128)} async-done(((f32[1,2,8,128,128]{4,3,2,1,0:T(8,128)}), f32[16,2,8,128,128]{4,3,2,1,0:T(8,128)}) %all-gather.3.cloned.1.call-update) | async-done | bytes 16777232 | tf_op jit(solution)/shard_map/all_gather | solution.py:31
  347.9 89.7 %while.28 = (s32[]{:T(128)}, f32[2,8,128,128]{2,3,1,0:T(8,128)}, s32[]{:T(128)}, f32[16,2,8,128,128]{4,3,2,1,0:T(8,128)}, s32[]{:T(128)}, /*index=5*/s32[]{:T(128)}, s32[]{}) while((s32[]{:T(128)}, f32[2,8,128,128]{2,3,1,0:T(8,128)}, s32[]{:T(128)}, f32[16,2,8,128,128]{4,3,2,1,0:T(8,128)}, s32[]{:T(128)}, /*index=5*/s32[]{:T(128)}, s32[]{}) %tuple.94), condition=%wide.region_4.6_spmd, body=%wide.region_3.5_spmd.sunk | while | flops 403177472 | bytes 8389227 | solution.py:40
  350.4 3.1 fusion.235
  356.0 3.1 fusion.235
  361.6 3.1 fusion.235
  367.2 3.1 fusion.235
  372.8 3.1 fusion.235
  378.4 3.1 fusion.235
  383.9 3.1 fusion.235
  389.5 3.1 fusion.235
  395.1 3.1 fusion.235
  400.7 3.1 fusion.235
  406.3 3.1 fusion.235
  411.9 3.1 fusion.235
  417.4 3.1 fusion.235
  423.0 3.1 fusion.235
  428.6 3.1 fusion.235
  434.2 3.1 fusion.235
  437.7 3.5 convolution_bitcast_fusion.5
  473.9 25.0 %all-reduce.16.cloned.1.call-done = f32[1,2,8,128,128]{4,3,2,1,0:T(8,128)} async-done(((f32[1,2,8,128,128]{4,3,2,1,0:T(8,128)}), f32[1,2,8,128,128]{4,3,2,1,0:T(8,128)}) %all-reduce.16.cloned.1.call-update) | async-done | bytes 1048592 | tf_op jit(solution)/shard_map/psum | solution.py:26
  509.4 6.4 fusion.65
  517.5 68.1 %psum.23 = f32[8,128]{1,0:T(8,128)S(1)} all-reduce(f32[8,128]{1,0:T(8,128)S(1)} %add.275), channel_id=1, replica_groups=mesh['dp'=4,'outer'=16,'inner'=2] {'dp','outer','inner'}, use_global_device_ids=true, to_apply=%region_16.19 | all-reduce | flops 1024 | bytes 8192 | tf_op jit(solution)/shard_map/psum | solution.py:246
  597.6 17.5 %all-gather.5.cloned.1.call-done = f32[16,2,8,128,128]{4,3,2,1,0:T(8,128)} async-done(((f32[1,2,8,128,128]{4,3,2,1,0:T(8,128)}), f32[16,2,8,128,128]{4,3,2,1,0:T(8,128)}) %all-gather.5.cloned.1.call-update) | async-done | bytes 16777232 | tf_op jit(solution)/shard_map/all_gather | solution.py:31
  615.1 56.1 %while.29 = (s32[]{:T(128)}, f32[2,8,128,128]{2,3,1,0:T(8,128)S(1)}, s32[]{:T(128)}, f32[16,2,8,128,128]{4,3,2,1,0:T(8,128)}, s32[]{:T(128)}, /*index=5*/s32[]{:T(128)}, s32[]{:T(128)}, s32[]{:T(128)}, s32[]{}) while((s32[]{:T(128)}, f32[2,8,128,128]{2,3,1,0:T(8,128)S(1)}, s32[]{:T(128)}, f32[16,2,8,128,128]{4,3,2,1,0:T(8,128)}, ...), condition=%wide.region_12.14_spmd, body=%wide.region_11.13_spmd.sunk | while | flops 403177472 | bytes 8388781 | solution.py:40
  671.3 3.1 convolution_bitcast_fusion.2
  693.5 3.1 convolution_negate_fusion.1
  711.1 44.5 %fusion.68 = bf16[128,2,8,128]{3,1,0,2:T(2,128)(2,1)S(1)} fusion(f32[8,128,2,128]{3,2,1,0:T(2,128)S(1)} %bitcast.296, f32[8,128,2]{2,1,0:T(8,128)} %copy.214, f32[128,2,8,128]{3,2,1,0:T(8,128)} %copy-done.14), kind=kOutput, calls=%fused_computation.98 | output fusion | flops 1837183 | bytes 2629632 | tf_op jit(solution)/shard_map/mul | solution.py:53
  (299 shorter events, 231.8 us)
Async XLA Ops:
  7.2 226.0 %all-reduce.14.cloned.1.call-start = ((), (), s32[]{:S(2)}) async-start(), calls=%async_computation | async-start | bytes 2097152 | tf_op jit(solution)/shard_map/psum | solution.py:26
  8.5 3.7 copy-start.14
  99.0 144.5 %copy-start.12 = (f32[8,128,256]{2,1,0:T(8,128)}, f32[8,128,256]{2,1,0:T(8,128)S(1)}, u32[]{:S(2)}) copy-start(f32[8,128,256]{2,1,0:T(8,128)S(1)} %fusion.73) | copy-start | bytes 3145732
  186.7 8.4 %copy-start.20 = (f32[8,128,128,1]{2,1,0,3:T(8,128)}, f32[8,128,128,1]{2,1,0,3:T(8,128)S(1)}, u32[]{:S(2)}) copy-start(f32[8,128,128,1]{2,1,0,3:T(8,128)S(1)} %fusion.55) | copy-start | bytes 1572868
  187.8 45.6 %copy-start.5 = (f32[1,8,128,128]{3,2,1,0:T(8,128)}, f32[1,8,128,128]{3,2,1,0:T(8,128)S(1)}, u32[]{:S(2)}) copy-start(f32[1,8,128,128]{3,2,1,0:T(8,128)S(1)} %stack_broadcast_in_dim.7) | copy-start | bytes 1572868
  193.2 3.3 copy-start.23
  195.1 5.2 collective-permute-start
  201.6 31.7 %copy-start.22 = (f32[1,8,128,128]{3,2,1,0:T(8,128)}, f32[1,8,128,128]{3,2,1,0:T(8,128)S(1)}, u32[]{:S(2)}) copy-start(f32[1,8,128,128]{3,2,1,0:T(8,128)S(1)} %get-tuple-element.266) | copy-start | bytes 1572868
  205.0 142.9 %all-gather.3.cloned.1.call-start = ((), (), s32[]{:S(2)}) async-start(), calls=%async_computation.1 | async-start | bytes 17825792 | tf_op jit(solution)/shard_map/all_gather | solution.py:31
  233.2 265.7 %all-reduce.16.cloned.1.call-start = ((), (), s32[]{:S(2)}) async-start(), calls=%async_computation.2 | async-start | bytes 2097152 | tf_op jit(solution)/shard_map/psum | solution.py:26
  240.0 4.9 copy-start.32
  241.3 3.6 copy-start.4
  242.4 209.9 %copy-start.25 = (f32[8,64,128]{2,1,0:T(8,128)}, f32[8,64,128]{2,1,0:T(8,128)S(1)}, u32[]{:S(2)}) copy-start(f32[8,64,128]{2,1,0:T(8,128)S(1)} %convolution_multiply_fusion.5) | copy-start | bytes 786436
  437.7 21.0 %copy-start.31 = (f32[8,64,128]{2,1,0:T(8,128)S(1)}, f32[8,64,128]{2,1,0:T(8,128)}, u32[]{:S(2)}) copy-start(f32[8,64,128]{2,1,0:T(8,128)} %convolution_subtract_fusion.7) | copy-start | bytes 786436
  437.7 22.0 %copy-start.6 = (f32[1,8,128,128]{3,2,1,0:T(8,128)S(1)}, f32[1,8,128,128]{3,2,1,0:T(8,128)}, u32[]{:S(2)}) copy-start(f32[1,8,128,128]{3,2,1,0:T(8,128)} %copy-done.5) | copy-start | bytes 1572868
  437.7 22.0 %copy-start.21 = (f32[8,128,128,1]{2,1,0,3:T(8,128)S(1)}, f32[8,128,128,1]{2,1,0,3:T(8,128)}, u32[]{:S(2)}) copy-start(f32[8,128,128,1]{2,1,0,3:T(8,128)} %copy-done.20) | copy-start | bytes 1572868
  437.7 23.2 %copy-start.30 = (f32[8,64,128]{2,1,0:T(8,128)S(1)}, f32[8,64,128]{2,1,0:T(8,128)}, u32[]{:S(2)}) copy-start(f32[8,64,128]{2,1,0:T(8,128)} %convolution_subtract_fusion.6) | copy-start | bytes 786436
  437.7 24.2 %copy-start.19 = (f32[8,128,128,1]{2,1,0,3:T(8,128)S(1)}, f32[8,128,128,1]{2,1,0,3:T(8,128)}, u32[]{:S(2)}) copy-start(f32[8,128,128,1]{2,1,0,3:T(8,128)} %fusion.50) | copy-start | bytes 1572868
  442.3 64.9 %copy-start = (f32[8,128,128]{2,1,0:T(8,128)}, f32[8,128,128]{2,1,0:T(8,128)S(1)}, u32[]{:S(2)}) copy-start(f32[8,128,128]{2,1,0:T(8,128)S(1)} %fusion.88) | copy-start | bytes 1572868
  444.9 60.1 %copy-start.2 = (f32[8,128,128]{2,1,0:T(8,128)}, f32[8,128,128]{2,1,0:T(8,128)S(1)}, u32[]{:S(2)}) copy-start(f32[8,128,128]{2,1,0:T(8,128)S(1)} %convolution_subtract_fusion.3) | copy-start | bytes 1572868
  445.9 7.1 copy-start.11
  448.5 3.8 copy-start.7
  465.1 4.9 collective-permute-start.1
  473.9 141.2 %all-gather.5.cloned.1.call-start = ((), (), s32[]{:S(2)}) async-start(), calls=%async_computation.3 | async-start | bytes 17825792 | tf_op jit(solution)/shard_map/all_gather | solution.py:31
  671.2 22.3 %copy-start.3 = (f32[8,128,128]{2,1,0:T(8,128)S(1)}, f32[8,128,128]{2,1,0:T(8,128)}, u32[]{:S(2)}) copy-start(f32[8,128,128]{2,1,0:T(8,128)} %copy-done.2) | copy-start | bytes 1572868
  671.2 29.2 %copy-start.1 = (f32[8,128,128]{2,1,0:T(8,128)S(1)}, f32[8,128,128]{2,1,0:T(8,128)}, u32[]{:S(2)}) copy-start(f32[8,128,128]{2,1,0:T(8,128)} %copy-done) | copy-start | bytes 1572868
  674.3 13.2 %copy-start.16 = (f32[2,8,128,128]{3,2,1,0:T(8,128)}, f32[2,8,128,128]{3,2,1,0:T(8,128)S(1)}, u32[]{:S(2)}) copy-start(f32[2,8,128,128]{3,2,1,0:T(8,128)S(1)} %convolution_bitcast_fusion.2) | copy-start | bytes 3145732
  674.4 29.1 %copy-start.8 = (f32[8,128,128]{2,1,0:T(8,128)S(1)}, f32[8,128,128]{2,1,0:T(8,128)}, u32[]{:S(2)}) copy-start(f32[8,128,128]{2,1,0:T(8,128)} %copy-done.7) | copy-start | bytes 1572868
  674.4 29.1 %copy-start.10 = (f32[1,8,128,128]{3,2,1,0:T(8,128)S(1)}, f32[1,8,128,128]{3,2,1,0:T(8,128)}, u32[]{:S(2)}) copy-start(f32[1,8,128,128]{3,2,1,0:T(8,128)} %copy-done.9) | copy-start | bytes 1572868
  674.4 33.0 %copy-start.33 = (f32[128,128]{1,0:T(8,128)S(1)}, f32[128,128]{1,0:T(8,128)}, u32[]{:S(2)}) copy-start(f32[128,128]{1,0:T(8,128)} %get-tuple-element.288) | copy-start | bytes 196612
  678.9 6.2 copy-start.15
  685.1 5.0 copy-start.24
  (9 other events, 11.1 us)
Sparse Core Ops, SparseCore 0:
  205.1 28.0 all-reduce.13
  235.5 112.3 all-gather.2
  474.0 24.8 all-reduce.15
  500.9 114.1 all-gather.4
where the time goes:
time: 773 us; the launch traced here: 764 us
  other arithmetic  223 us (29%)
  matrix products  188 us (24%)
  waiting for transfers between devices  177 us (23%)
  local copies, waits for them, and re-layouts  85.9 us (11%)
  blocking collectives  68.1 us (9%)
  between operations  15 us (2%)
    dot_general x83, matrix products, product(): jnp.einsum(spec, left, right, precision=EXACT, preferred_element_type=jnp...  180 us
    another operation x3, other arithmetic, stretch_factors(): solved = jax.scipy.linalg.solve_triangular(lower_mat, rhs, lower=True)  159 us
    all_gather x2, waiting for transfers between devices, prefix(): everything = lax.all_gather(shard, axis)  118 us
    psum x1, blocking collectives, on_device(): total = lax.psum(gain_sum, ('dp', 'outer', 'inner'))  68.1 us
    psum x2, waiting for transfers between devices, spread(): return lax.psum(kept, axis)  53.1 us
    mul x2, other arithmetic, unit_back(): unit * jnp.sum(unit * grad, axis=-1, keepdims=True)  50.9 us
    slice x34, local copies, waits for them, and re-layouts, compose(): return through + jnp.stack([jnp.zeros_like(later[1]), later[1]])  34.6 us
    while x64, local copies, waits for them, and re-layouts  27 us
  transfers between devices with their start and end apart: 6, of which 6 were waited for; matrix products, arithmetic and copies ran while one was open for 6% of the time, Pallas kernels for 0%

commit v1 on v0

v1 whole, which is shorter than its diff:
```python
import functools
import math

import jax
import jax.numpy as jnp
from jax import lax
from jax.experimental import pallas as pl
from jax.experimental.pallas import tpu as pltpu
from jax.sharding import PartitionSpec as P

HEADS = 8
DIM = 128
HALF = 64
GROUP = 2
EPS_KEY = 1e-06
EPS_OUT = 1e-05
F32 = jnp.float32
BF16 = jnp.bfloat16
MESH = pl.DeviceIdType.MESH
VMEM = pl.BlockSpec(memory_space=pltpu.VMEM)
LIMIT = 48 * 1024 * 1024


def split(x):
    high = x.astype(BF16)
    return high, (x - high.astype(F32)).astype(BF16)


def raw_dot(left, right, dims):
    return lax.dot_general(left, right, (dims, ((), ())), preferred_element_type=F32)


def folded(wide):
    half = wide.shape[1] // 2
    return wide[:, :half] + wide[:, half:]


def nn(a, b):
    lhs = jnp.concatenate(a, axis=1)
    rhs = jnp.concatenate(b, axis=1)
    return folded(raw_dot(lhs, jnp.concatenate([rhs, rhs], axis=0), ((1,), (0,))))


def nt(a, b):
    lhs = jnp.concatenate(a, axis=1)
    rhs = jnp.concatenate(b, axis=0)
    return folded(raw_dot(lhs, jnp.concatenate([rhs, rhs], axis=1), ((1,), (1,))))


def tn(a, b):
    lhs = jnp.concatenate(a, axis=0)
    rhs = jnp.concatenate(b, axis=1)
    return folded(raw_dot(lhs, jnp.concatenate([rhs, rhs], axis=0), ((0,), (0,))))


def stacked(*pairs):
    return tuple(jnp.concatenate(part, axis=0) for part in zip(*pairs))


def beside(*pairs):
    return tuple(jnp.concatenate(part, axis=1) for part in zip(*pairs))


def inv_norm(x):
    return lax.rsqrt(jnp.sum(x * x, axis=1, keepdims=True) + EPS_KEY)


def places():
    row = lax.broadcasted_iota(jnp.int32, (DIM, DIM), 0)
    col = lax.broadcasted_iota(jnp.int32, (DIM, DIM), 1)

    def order(n):
        return jnp.where(n < HALF, 2 * n, 2 * n - (DIM - 1))

    return row, col, order(row), order(col)


def read_mask(col):
    token = lax.broadcasted_iota(jnp.int32, (HALF, DIM), 0)
    return jnp.where(col[:HALF] < HALF, col[:HALF], col[:HALF] - HALF) <= token


def rows_of(first, second, block, head):
    at = slice(block * HALF, (block + 1) * HALF)
    cols = slice(head * DIM, (head + 1) * DIM)
    return jnp.concatenate([first[at, cols], second[at, cols]], axis=0)


def tokens_of(ref, block, head):
    return ref[block * HALF : (block + 1) * HALF, head * DIM : (head + 1) * DIM]


def maps_kernel(q, k0, k1, v0, v1, rate, t_dev, o_dev, q_dev, y_dev, w_out, u_out, g_out, z_out, t_out, o_out, qe_out):
    row, col, row_at, col_at = places()
    eye = row == col
    strict = col_at < row_at
    reads = read_mask(col)
    many = [(h, b) for h in range(GROUP) for b in range(2)]
    count = len(many)
    key, val, query, ratecol, raterow = [], [], [], [], []
    for h, b in many:
        kr = rows_of(k0, k1, b, h).astype(F32)
        key.append(kr * inv_norm(kr))
        val.append(rows_of(v0, v1, b, h))
        qr = tokens_of(q, b, h).astype(F32)
        query.append(qr * inv_norm(qr))
        r = rate[h, b : b + 1, :]
        raterow.append(r)
        ratecol.append(jnp.sum(jnp.where(eye, r, 0.0), axis=1, keepdims=True))
    keys = [split(x) for x in key]
    both = [nt(stacked(keys[i], split(query[i])), keys[i]) for i in range(count)]
    lower = [split(jnp.where(strict, ratecol[i] * both[i][:DIM], 0.0)) for i in range(count)]
    scores = [split(jnp.where(reads, both[i][DIM:], 0.0)) for i in range(count)]

    def level(s):
        shift = s.bit_length() - 1
        rb, cb = row_at >> shift, col_at >> shift
        return ((rb >> 1) == (cb >> 1)) & ((rb & 1) == 1) & ((cb & 1) == 0)

    def masked(pair, mask):
        return tuple(jnp.where(mask, x.astype(F32), 0.0).astype(BF16) for x in pair)

    one = jnp.where(eye, 1.0, 0.0)
    first = level(1)
    inverse = [one - jnp.where(first, ratecol[i] * both[i][:DIM], 0.0) for i in range(count)]
    s = 2
    while s < DIM:
        mask = level(s)
        halves = [split(x) for x in inverse]
        inner = [split(nn(masked(lower[i], mask), halves[i])) for i in range(count)]
        inverse = [inverse[i] - nn(halves[i], inner[i]) for i in range(count)]
        s *= 2
    scaled = [split(inverse[i] * raterow[i]) for i in range(count)]
    zero = jnp.zeros((DIM, DIM), BF16)
    pack = [beside(keys[i], (val[i], zero)) for i in range(count)]
    solved = [nn(scaled[i], pack[i]) for i in range(count)]
    z = [nn(scores[i], scaled[i]) for i in range(count)]
    gmat = [tn(scaled[i], keys[i]) for i in range(count)]
    zr = [nn(split(z[i]), pack[i]) for i in range(count)]
    move = [tn(split(solved[i]), keys[i]) for i in range(count)]
    trans = [one - move[i][:DIM] for i in range(count)]
    offs = [move[i][DIM:] for i in range(count)]
    qe = [query[i] - zr[i][:, :DIM] for i in range(count)]
    y = [zr[i][:, DIM:] for i in range(count)]
    for i, (h, b) in enumerate(many):
        w_out[h, b] = solved[i][:, :DIM]
        u_out[h, b] = solved[i][:, DIM:]
        g_out[h, b] = gmat[i]
        z_out[h, b] = z[i]
        t_out[h, b] = trans[i]
    for h in range(GROUP):
        a, b = 2 * h, 2 * h + 1
        ta, tb = split(trans[a]), split(trans[b])
        oa, qb = split(offs[a]), split(qe[b])
        through = nn(stacked(ta, oa), tb)
        t_dev[h] = through[:DIM]
        o_dev[h] = through[DIM:] + offs[b]
        back = nt(qb, stacked(ta, oa))
        q_dev[h] = jnp.concatenate([qe[a], back[:, :DIM]], axis=0)
        y_dev[h] = jnp.concatenate([y[a], y[b] + back[:, DIM:]], axis=0)
        o_out[h] = offs[a]
        qe_out[h] = qe[b]


def shape(*dims, dtype=F32):
    return jax.ShapeDtypeStruct(dims, dtype)


def head_spec(*rest):
    return pl.BlockSpec((GROUP, *rest), lambda i: (i,) + (0,) * len(rest))


def wide_spec(offset=0):
    return pl.BlockSpec((DIM, GROUP * DIM), lambda i: (0, i + offset))


def state_maps(q, k, v, rate):
    steps = HEADS // GROUP
    square, pair, thin = (DIM, DIM), (2, DIM, DIM), (2, HALF, DIM)
    outs = [square, square, square, square, pair, pair, pair, thin, pair, square, (HALF, DIM)]
    return pl.pallas_call(
        maps_kernel,
        grid=(steps,),
        in_specs=[wide_spec(), wide_spec(), wide_spec(steps), wide_spec(), wide_spec(steps), head_spec(2, DIM)],
        out_specs=[head_spec(*s) for s in outs],
        out_shape=[shape(HEADS, *s) for s in outs],
        compiler_params=pltpu.CompilerParams(vmem_limit_bytes=LIMIT),
    )(q, k, k, v, v, rate)


def place():
    return 2 * lax.axis_index("outer") + lax.axis_index("inner")


def device(d):
    return {"outer": lax.div(d, 2), "inner": lax.rem(d, 2)}


def greet(n, others):
    barrier = pltpu.get_barrier_semaphore()
    me = place()

    def tell(i, c):
        pl.semaphore_signal(barrier, inc=1, device_id=device(lax.rem(me + i, n)), device_id_type=MESH)
        return c

    lax.fori_loop(1, n, tell, 0)
    for peer in others:
        pl.semaphore_signal(barrier, inc=1, device_id=peer, device_id_type=MESH)
    pl.semaphore_wait(barrier, n - 1 + len(others))


def to(src, dst, send, recv, target):
    return pltpu.make_async_remote_copy(
        src_ref=src, dst_ref=dst, send_sem=send, recv_sem=recv, device_id=target, device_id_type=MESH
    )


def forward_kernel(n, t_dev, o_dev, t_all, state, o_all, s_all, st, rt, so, ro, ss, rs):
    me = place()
    greet(n, ())

    def put(i, c):
        d = lax.rem(me + i, n)
        to(t_dev.at[lax.div(d, 4)], t_all.at[me], st.at[d], rt.at[me], device(d)).start()
        to(o_dev.at[d], o_all.at[me], so.at[d], ro.at[me], device(d)).start()
        return c

    lax.fori_loop(1, n, put, 0)
    t_all[me] = t_dev[lax.div(me, 4)]
    o_all[me] = o_dev[me]

    def step(p, now):
        @pl.when(p != me)
        def _():
            to(t_dev.at[0], t_all.at[p], st.at[p], rt.at[p], device(p)).wait_recv()
            to(o_dev.at[0], o_all.at[p], so.at[p], ro.at[p], device(p)).wait_recv()

        s_all[p] = now

        @pl.when(p != me)
        def _():
            to(s_all.at[p], state.at[me], ss.at[p], rs.at[me], device(p)).start()

        return nn(split(now), split(t_all[p])) + o_all[p]

    lax.fori_loop(0, n, step, jnp.zeros((DIM // 4, DIM), F32))
    state[me] = s_all[me]

    def finish(i, c):
        d = lax.rem(me + i, n)
        to(s_all.at[d], state.at[d], ss.at[d], rs.at[d], device(d)).wait()
        to(t_dev.at[0], t_all.at[d], st.at[d], rt.at[d], device(d)).wait_send()
        to(o_dev.at[0], o_all.at[d], so.at[d], ro.at[d], device(d)).wait_send()
        return c

    lax.fori_loop(1, n, finish, 0)


def dma(n):
    return pltpu.SemaphoreType.DMA((n,))


def forward_scan(t_dev, o_dev, n):
    return pl.pallas_call(
        functools.partial(forward_kernel, n),
        in_specs=[VMEM, VMEM],
        out_specs=[VMEM, VMEM],
        out_shape=[shape(n, DIM, DIM), shape(n, DIM // 4, DIM)],
        scratch_shapes=[pltpu.VMEM((n, DIM // 4, DIM), F32), pltpu.VMEM((n, DIM // 4, DIM), F32)] + [dma(n)] * 6,
        compiler_params=pltpu.CompilerParams(collective_id=0, has_side_effects=True, vmem_limit_bytes=LIMIT),
    )(t_dev, o_dev)


def middle_kernel(q_dev, y_dev, state, cotan, gain, d_out, source):
    for h in range(GROUP):
        cols = slice(h * DIM, (h + 1) * DIM)
        cot = cotan[:, cols].astype(F32)
        qd = split(q_dev[h])
        out = nt(qd, split(state[h])) + y_dev[h]
        scale = lax.rsqrt(jnp.mean(out * out, axis=1, keepdims=True) + EPS_OUT)
        normed = out * scale
        scaled = cot * gain[h]
        grad = scale * (scaled - normed * jnp.mean(normed * scaled, axis=1, keepdims=True))
        d_out[h] = grad
        src = tn(split(grad), qd)
        part = jnp.sum(cot * normed, axis=0, keepdims=True)
        for quarter in range(4):
            source[h, quarter, 0:32] = src[quarter * 32 : quarter * 32 + 32]
            source[h, quarter, 32:40] = jnp.broadcast_to(part, (8, DIM))


def middle(q_dev, y_dev, state, cotan, gain):
    square = head_spec(DIM, DIM)
    return pl.pallas_call(
        middle_kernel,
        grid=(HEADS // GROUP,),
        in_specs=[square, square, square, wide_spec(), head_spec(1, DIM)],
        out_specs=[square, head_spec(4, 40, DIM)],
        out_shape=[shape(HEADS, DIM, DIM), shape(HEADS, 4, 40, DIM)],
        compiler_params=pltpu.CompilerParams(vmem_limit_bytes=LIMIT),
    )(q_dev, y_dev, state, cotan, gain)


def backward_kernel(n, ways, source, t_all, adjoint, total, got, a_all, g_all, sx, rx, sa, ra, sd, rd, sg, rg):
    me = place()
    dp = lax.axis_index("dp")
    peers = [{"dp": lax.rem(dp + i, ways)} for i in range(1, ways)]
    greet(n, peers)

    def put(i, c):
        d = lax.rem(me - i + n, n)
        to(source.at[d], got.at[me], sx.at[d], rx.at[me], device(d)).start()
        return c

    lax.fori_loop(1, n, put, 0)
    got[me] = source[me]

    def step(i, carry):
        now, gains = carry
        p = n - 1 - i

        @pl.when(p != me)
        def _():
            to(source.at[0], got.at[p], sx.at[p], rx.at[p], device(p)).wait_recv()

        a_all[p] = now

        @pl.when(p != me)
        def _():
            to(a_all.at[p], adjoint.at[me], sa.at[p], ra.at[me], device(p)).start()

        return nt(split(now), split(t_all[p])) + got[p, 0:32], gains + got[p, 32:40]

    _, gains = lax.fori_loop(0, n, step, (jnp.zeros((DIM // 4, DIM), F32), jnp.zeros((8, DIM), F32)))
    adjoint[me] = a_all[me]
    g_all[dp] = gains
    for i in range(1, ways):
        other = lax.rem(dp + i, ways)
        to(g_all.at[dp], g_all.at[dp], sd.at[other], rd.at[dp], {"dp": other}).start()
    for i in range(1, ways):
        other = lax.rem(dp + i, ways)
        to(g_all.at[other], g_all.at[other], sd.at[other], rd.at[other], {"dp": other}).wait()
    summed = g_all[0]
    for i in range(1, ways):
        summed = summed + g_all[i]
    head = lax.div(me, 4)

    @pl.when(lax.rem(me, 4) == 0)
    def _():
        total[head] = summed

        def give(i, c):
            d = lax.rem(me + i, n)
            to(total.at[head], total.at[head], sg.at[d], rg.at[head], device(d)).start()
            return c

        lax.fori_loop(1, n, give, 0)

        def gone(i, c):
            d = lax.rem(me + i, n)
            to(total.at[head], total.at[head], sg.at[d], rg.at[head], device(d)).wait_send()
            return c

        lax.fori_loop(1, n, gone, 0)

    for h in range(HEADS):

        @pl.when(me != 4 * h)
        def _(h=h):
            to(total.at[h], total.at[h], sg.at[h], rg.at[h], device(4 * h)).wait_recv()

    def finish(i, c):
        d = lax.rem(me + i, n)
        to(a_all.at[d], adjoint.at[d], sa.at[d], ra.at[d], device(d)).wait()
        to(source.at[d], got.at[d], sx.at[d], rx.at[d], device(d)).wait_send()
        return c

    lax.fori_loop(1, n, finish, 0)


def backward_scan(source, t_all, n, ways):
    return pl.pallas_call(
        functools.partial(backward_kernel, n, ways),
        in_specs=[VMEM, VMEM],
        out_specs=[VMEM, VMEM],
        out_shape=[shape(n, DIM // 4, DIM), shape(HEADS, 8, DIM)],
        scratch_shapes=[
            pltpu.VMEM((n, 40, DIM), F32),
            pltpu.VMEM((n, DIM // 4, DIM), F32),
            pltpu.VMEM((ways, 8, DIM), F32),
        ]
        + [dma(n)] * 4
        + [dma(ways)] * 2
        + [dma(n), dma(HEADS)],
        compiler_params=pltpu.CompilerParams(collective_id=1, has_side_effects=True, vmem_limit_bytes=LIMIT),
    )(source, t_all)


def unit_back(unit, inv, grad):
    return inv * (grad - unit * jnp.sum(unit * grad, axis=1, keepdims=True))


def final_kernel(
    q, k0, k1, state, adjoint, grad, w_in, u_in, g_in, z_in, t_in, o_in, qe_in, gq_out, gk0, gk1, gv0, gv1
):
    row, col, row_at, col_at = places()
    strict = col_at < row_at
    reads = read_mask(col)
    many = [(h, b) for h in range(GROUP) for b in range(2)]
    count = len(many)
    key, kinv, query, qinv, states, adjoints, do = [], [], [], [], [], [], []
    for h in range(GROUP):
        ta, tb = split(t_in[h, 0]), split(t_in[h, 1])
        s0, a1 = split(state[h]), split(adjoint[h])
        do0, do1 = split(grad[h, :HALF]), split(grad[h, HALF:])
        s1 = split(nn(s0, ta) + o_in[h])
        a0 = split(nt(a1, tb) + tn(do1, split(qe_in[h])))
        states += [s0, s1]
        adjoints += [a0, a1]
        do += [do0, do1]
        for b in range(2):
            kr = rows_of(k0, k1, b, h).astype(F32)
            kinv.append(inv_norm(kr))
            key.append(kr * kinv[-1])
            qr = tokens_of(q, b, h).astype(F32)
            qinv.append(inv_norm(qr))
            query.append(qr * qinv[-1])
    keys = [split(x) for x in key]
    update = [split(u_in[many[i]] - nt(split(w_in[many[i]]), states[i])) for i in range(count)]
    target = [tn(split(z_in[many[i]]), do[i]) + nt(split(g_in[many[i]]), adjoints[i]) for i in range(count)]
    less = [split(-x) for x in target]
    pair = [stacked(do[i], less[i]) for i in range(count)]
    inner = [nt(pair[i], update[i]) for i in range(count)]
    d_scores = [split(jnp.where(reads, inner[i][:HALF], 0.0)) for i in range(count)]
    d_gram = [jnp.where(strict, inner[i][HALF:], 0.0) for i in range(count)]
    d_gram = [split(x + x.T) for x in d_gram]
    by_state = [nn(pair[i], states[i]) for i in range(count)]
    by_key = [nn(stacked(d_scores[i], d_gram[i]), keys[i]) for i in range(count)]
    by_adj = [nn(update[i], adjoints[i]) for i in range(count)]
    by_query = [tn(d_scores[i], split(query[i])) for i in range(count)]
    for i, (h, b) in enumerate(many):
        both = by_state[i] + by_key[i]
        gq = unit_back(query[i], qinv[i], both[:HALF]).astype(BF16)
        gk = unit_back(key[i], kinv[i], both[HALF:] + by_adj[i] + by_query[i]).astype(BF16)
        gv = target[i].astype(BF16)
        at = slice(b * HALF, (b + 1) * HALF)
        cols = slice(h * DIM, (h + 1) * DIM)
        gq_out[at, cols] = gq
        gk0[at, cols] = gk[:HALF]
        gk1[at, cols] = gk[HALF:]
        gv0[at, cols] = gv[:HALF]
        gv1[at, cols] = gv[HALF:]


def final(q, k, state, adjoint, grad, w_in, u_in, g_in, z_in, t_in, o_in, qe_in):
    steps = HEADS // GROUP
    square, pair, thin = head_spec(DIM, DIM), head_spec(2, DIM, DIM), head_spec(2, HALF, DIM)
    return pl.pallas_call(
        final_kernel,
        grid=(steps,),
        in_specs=[wide_spec(), wide_spec(), wide_spec(steps), square, square, square]
        + [pair, pair, pair, thin, pair, square, head_spec(HALF, DIM)],
        out_specs=[wide_spec()] * 5,
        out_shape=[shape(DIM, HEADS * DIM, dtype=BF16)] * 5,
        compiler_params=pltpu.CompilerParams(vmem_limit_bytes=LIMIT),
    )(q, k, k, state, adjoint, grad, w_in, u_in, g_in, z_in, t_in, o_in, qe_in)


def on_device(queries, keys, values, betas, grad_out, gain):
    n = lax.axis_size("outer") * lax.axis_size("inner")
    ways = lax.axis_size("dp")
    q = queries[0]
    k = keys[0].reshape(DIM, 2 * HEADS * DIM)
    v = values[0].reshape(DIM, 2 * HEADS * DIM)
    rate = betas[0].reshape(HEADS, 2, 2, HALF).transpose(0, 2, 1, 3).reshape(HEADS, 2, DIM)
    t_dev, o_dev, q_dev, y_dev, w, u, g, z, t_blk, o_blk, qe = state_maps(q, k, v, rate)
    t_all, state = forward_scan(t_dev, o_dev.reshape(n, DIM // 4, DIM), n)
    state = state.reshape(HEADS, DIM, DIM)
    grad, source = middle(q_dev, y_dev, state, grad_out[0], gain.reshape(HEADS, 1, DIM))
    adjoint, total = backward_scan(source.reshape(n, 40, DIM), t_all, n, ways)
    adjoint = adjoint.reshape(HEADS, DIM, DIM)
    gq, gk0, gk1, gv0, gv1 = final(q, k, state, adjoint, grad, w, u, g, z, t_blk, o_blk, qe)
    grad_k = jnp.stack([gk0, gk1], axis=1)[None]
    grad_v = jnp.stack([gv0, gv1], axis=1)[None]
    gain_grad = total[:, 0, :].reshape(HEADS * DIM) * (1.0 / math.sqrt(DIM * n * ways))
    return gq[None], grad_k, grad_v, gain_grad


def solution(mesh):
    seq = ("outer", "inner")
    return jax.shard_map(
        on_device,
        mesh=mesh,
        in_specs=(
            P("dp", seq, None),
            P("dp", seq, None, None),
            P("dp", seq, None, None),
            P("dp", None, None, seq),
            P("dp", seq, None),
            P(),
        ),
        out_specs=(P("dp", seq, None), P("dp", seq, None, None), P("dp", seq, None, None), P()),
        check_vma=False,
    )
```

time: 773 us -> 123 us (0.16); the launches traced: 764 us -> 122 us
  other arithmetic: 223 us -> 0.7 us
  matrix products: 188 us -> 0 us
  waiting for transfers between devices: 177 us -> 0 us
  Pallas kernels: 0 us -> 115 us
  local copies, waits for them, and re-layouts: 85.9 us -> 5.96 us
  blocking collectives: 68.1 us -> 0 us
  between operations: 15 us -> 0.72 us
    dot_general x83 -> x0, matrix products: 180 us -> none  [product(): jnp.einsum(spec, left, right, precision=EXACT, preferred_element_type=jnp...]
    another operation x3 -> x0, other arithmetic: 159 us -> none  [stretch_factors(): solved = jax.scipy.linalg.solve_triangular(lower_mat, rhs, lower=True)]
    all_gather x2 -> x0, waiting for transfers between devices: 118 us -> none  [prefix(): everything = lax.all_gather(shard, axis)]
    pallas_call x0 -> x5, Pallas kernels: none -> 115 us  [the longest x1 56.5 us: forward_scan(): pl.pallas_call(functools.partial(forward_kernel, n), in_specs=[VMEM, VMEM...]
    psum x1 -> x0, blocking collectives: 68.1 us -> none  [on_device(): total = lax.psum(gain_sum, ('dp', 'outer', 'inner'))]
    mul x7 -> x1, other arithmetic: 55.8 us -> 0.6 us  [on_device(): total[:, 0, :].reshape(HEADS * DIM) * (1.0 / math.sqrt(DIM * n * ways))]
    psum x2 -> x0, waiting for transfers between devices: 53.1 us -> none  [spread(): return lax.psum(kept, axis)]
    slice x37 -> x0, local copies, waits for them, and re-layouts: 34.7 us -> none  [the longest x34 34.6 us: compose(): return through + jnp.stack([jnp.zeros_like(later[1]), later[1]])]
  transfers between devices with their start and end apart: 6 -> 0, of which waited for: 6 -> 0; matrix products, arithmetic and copies ran while one was open for 6% -> 0% of each run, Pallas kernels for 0% -> 0%
where the time goes in v1:
time: 123 us; the launch traced here: 122 us
  Pallas kernels  115 us (93%)
  local copies, waits for them, and re-layouts  5.96 us (5%)
    pallas_call x1, Pallas kernels, forward_scan(): pl.pallas_call(functools.partial(forward_kernel, n), in_specs=[VMEM, VMEM...  56.5 us
    pallas_call x1, Pallas kernels, backward_scan(): pl.pallas_call(functools.partial(backward_kernel, n, ways), in_specs=[VME...  32.4 us
    pallas_call x1, Pallas kernels, state_maps(): pl.pallas_call(maps_kernel, grid=(steps,), in_specs=[wide_spec(), wide_sp...  14.9 us
    pallas_call x1, Pallas kernels, final(): pl.pallas_call(final_kernel, grid=(steps,), in_specs=[wide_spec(), wide_s...  7.08 us
    unnamed x10, local copies, waits for them, and re-layouts  5.04 us
    pallas_call x1, Pallas kernels, middle(): pl.pallas_call(middle_kernel, grid=(HEADS // GROUP,), in_specs=[square, s...  4.11 us

profile of v1, /device:TPU:1, one launch (start us, length us, event | category | flops | bytes accessed | tf_op | source)
XLA Modules:
  0.0 122.4 jit_solution(4827368597787824208)
XLA Ops:
  0.6 0.0 copy-start
  0.6 0.8 reshape_squeeze.12
  1.5 0.1 reshape.28.rate
  1.6 1.2 copy.13
  2.7 0.0 copy-start.1
  2.7 0.0 copy-start.2
  2.8 1.2 copy.14
  4.0 0.0 copy-done
  4.0 14.9 %shard_map.93 = (f32[8,128,128]{2,1,0:T(8,128)S(1)}, f32[8,128,128]{2,1,0:T(8,128)S(1)}, f32[8,128,128]{2,1,0:T(8,128)S(1)}, f32[8,128,128]{2,1,0:T(8,128)S(1)},...) custom-call(bf16[128,1024]{1,0:T(8,128)(2,1)S(1)} %bitcast.34, ...), custom_call_target="tpu_custom_call" | custom-call | tf_op jit(solution)/shard_map/pallas_call | solution.py:181
  18.9 56.5 %shard_map.94 = (f32[32,128,128]{2,1,0:T(8,128)S(1)}, f32[32,32,128]{2,1,0:T(8,128)S(1)}) custom-call(f32[8,128,128]{2,1,0:T(8,128)S(1)} %get-tuple-element.26.t_dev, f32[32,32,128]{2,1,0:T(8,128)S(1)} %bitcast.38), custom_call_target="tpu_custom_call" | custom-call | tf_op jit(solution)/shard_map/pallas_call | solution.py:265
  75.4 0.0 copy-done.1
  75.4 0.0 copy-done.2
  75.4 4.1 %shard_map.95 = (f32[8,128,128]{2,1,0:T(8,128)S(1)}, f32[8,4,40,128]{3,2,1,0:T(8,128)S(1)}) custom-call(f32[8,128,128]{2,1,0:T(8,128)S(1)} %get-tuple-element.29.q_dev, f32[8,128,128]{2,1,0:T(8,128)S(1)} %get-tuple-element.30.y_dev, f32[8,128,128]{2,1,0:T(8,128)S(1)} %bitcast.32, bf16[128,1024]{1,0:T(8,128)(2,1)S(1)} %bitcast.39, f32[8,1,128]{2,1,0:T(1,128)S(1)} %bitcast.44), custom_call_target="tpu_custom_call" | custom-call | tf_op jit(solution)/shard_map/pallas_call | solution.py:295
  79.5 32.4 %shard_map.96 = (f32[32,32,128]{2,1,0:T(8,128)S(1)}, f32[8,8,128]{2,1,0:T(8,128)S(1)}) custom-call(f32[32,40,128]{2,1,0:T(8,128)S(1)} %bitcast.36, f32[32,128,128]{2,1,0:T(8,128)S(1)} %get-tuple-element.32.t_all), custom_call_target="tpu_custom_call" | custom-call | tf_op jit(solution)/shard_map/pallas_call | solution.py:383
  112.0 7.1 %shard_map.97 = (bf16[128,1024]{1,0:T(8,128)(2,1)}, bf16[128,1024]{1,0:T(8,128)(2,1)S(1)}, bf16[128,1024]{1,0:T(8,128)(2,1)S(1)}, bf16[128,1024]{1,0:T(8,128)(2,1)S(1)}, bf16[128,1024]{1,0:T(8,128)(2,1)S(1)}) custom-call(bf16[128,1024]{1,0:T(8,128)(2,1)S(1)} %bitcast.35, bf16[128,2048]{1,0:T(8,128)(2,1)S(1)} %bitcast.28, bf16[128,2048]{1,0:T(8,128)(2,1)S(1)} %bitcast.29, ...), custom_call_target="tpu_custom_call" | custom-call | tf_op jit(solution)/shard_map/pallas_call | solution.py:459
  119.1 0.1 maximum_bitcast_fusion
  119.1 1.3 %copy.11 = bf16[1,128,2,1024]{3,2,1,0:T(2,128)(2,1)} copy(bf16[1,128,2,1024]{3,1,2,0:T(8,128)(2,1)S(1)} %maximum_bitcast_fusion) | data formatting | bytes 1048576
  120.5 0.6 slice_multiply_fusion
  121.0 0.1 maximum_bitcast_fusion.1
  121.1 1.3 %copy.12 = bf16[1,128,2,1024]{3,2,1,0:T(2,128)(2,1)} copy(bf16[1,128,2,1024]{3,1,2,0:T(8,128)(2,1)S(1)} %maximum_bitcast_fusion.1) | data formatting | bytes 1048576
  (1 shorter events, 0.0 us)
Async XLA Ops:
  0.6 3.3 %copy-start = (bf16[1,128,1024]{2,1,0:T(8,128)(2,1)S(1)}, bf16[1,128,1024]{2,1,0:T(8,128)(2,1)}, u32[]{:S(2)}) copy-start(bf16[1,128,1024]{2,1,0:T(8,128)(2,1)} %param.6) | copy-start | bytes 786436
  2.7 72.7 %copy-start.1 = (bf16[1,128,1024]{2,1,0:T(8,128)(2,1)S(1)}, bf16[1,128,1024]{2,1,0:T(8,128)(2,1)}, u32[]{:S(2)}) copy-start(bf16[1,128,1024]{2,1,0:T(8,128)(2,1)} %param.10) | copy-start | bytes 786436
  2.7 72.7 %copy-start.2 = (f32[1024]{0:T(1024)S(1)}, f32[1024]{0:T(1024)}, u32[]{:S(2)}) copy-start(f32[1024]{0:T(1024)} %param.11) | copy-start | bytes 12292

commit v2 on v1

v2 whole, which is shorter than its diff:
```python
import functools
import math

import jax
import jax.numpy as jnp
from jax import lax
from jax.experimental import pallas as pl
from jax.experimental.pallas import tpu as pltpu
from jax.sharding import PartitionSpec as P

HEADS = 8
DIM = 128
HALF = 64
GROUP = 2
RUN = 4
EPS_KEY = 1e-06
EPS_OUT = 1e-05
F32 = jnp.float32
BF16 = jnp.bfloat16
MESH = pl.DeviceIdType.MESH
VMEM = pl.BlockSpec(memory_space=pltpu.VMEM)
LIMIT = 48 * 1024 * 1024


def split(x):
    high = x.astype(BF16)
    return high, (x - high.astype(F32)).astype(BF16)


def raw_dot(left, right, dims):
    return lax.dot_general(left, right, (dims, ((), ())), preferred_element_type=F32)


def folded(wide):
    half = wide.shape[1] // 2
    return wide[:, :half] + wide[:, half:]


def nn(a, b):
    lhs = jnp.concatenate(a, axis=1)
    rhs = jnp.concatenate(b, axis=1)
    return folded(raw_dot(lhs, jnp.concatenate([rhs, rhs], axis=0), ((1,), (0,))))


def nt(a, b):
    lhs = jnp.concatenate(a, axis=1)
    rhs = jnp.concatenate(b, axis=0)
    return folded(raw_dot(lhs, jnp.concatenate([rhs, rhs], axis=1), ((1,), (1,))))


def tn(a, b):
    lhs = jnp.concatenate(a, axis=0)
    rhs = jnp.concatenate(b, axis=1)
    return folded(raw_dot(lhs, jnp.concatenate([rhs, rhs], axis=0), ((0,), (0,))))


def nn_sum(*terms):
    lhs = jnp.concatenate([x for a, _ in terms for x in a], axis=1)
    rhs = []
    for _, b in terms:
        rhs += [jnp.concatenate(b, axis=1)] * 2
    return folded(raw_dot(lhs, jnp.concatenate(rhs, axis=0), ((1,), (0,))))


def stacked(*pairs):
    return tuple(jnp.concatenate(part, axis=0) for part in zip(*pairs))


def beside(*pairs):
    return tuple(jnp.concatenate(part, axis=1) for part in zip(*pairs))


def inv_norm(x):
    return lax.rsqrt(jnp.sum(x * x, axis=1, keepdims=True) + EPS_KEY)


def places():
    row = lax.broadcasted_iota(jnp.int32, (DIM, DIM), 0)
    col = lax.broadcasted_iota(jnp.int32, (DIM, DIM), 1)

    def order(n):
        return jnp.where(n < HALF, 2 * n, 2 * n - (DIM - 1))

    return row, col, order(row), order(col)


def read_mask(col):
    token = lax.broadcasted_iota(jnp.int32, (HALF, DIM), 0)
    return jnp.where(col[:HALF] < HALF, col[:HALF], col[:HALF] - HALF) <= token


def put(ref, at, pair):
    ref[(0, *at)] = pair[0]
    ref[(1, *at)] = pair[1]


def get(ref, *at):
    return ref[(0, *at)], ref[(1, *at)]


def joined(pair):
    return pair[0].astype(F32) + pair[1].astype(F32)


def columns(head, part=0):
    return pl.ds(pl.multiple_of((part * HEADS + head) * DIM, DIM), DIM)


def tokens(block):
    return slice(block * HALF, (block + 1) * HALF)


def two_keys(ref, block, head):
    return jnp.concatenate([ref[tokens(block), columns(head, j)] for j in range(2)], axis=0)


def to(src, dst, send, recv, target):
    return pltpu.make_async_remote_copy(
        src_ref=src, dst_ref=dst, send_sem=send, recv_sem=recv, device_id=target, device_id_type=MESH
    )


def device(d):
    return {"outer": lax.div(d, 2), "inner": lax.rem(d, 2)}


def layer_kernel(
    n, ways,
    q, k, v, rate, cotan, gain,
    gq_out, gk_out, gv_out, total,
    t_dev, o_dev, q_dev, y_dev, knp, qnp, kinv, qinv, wp, u, gp, zp, tp, o_blk, qep,
    t_all, o_all, runs, local, s_all, state, dop, source, got, a_all, adjoint, g_all,
    sp, upd, part, hold, src1,
    st, rt, sf, rf, so, ro, ss, rs, sx, rx, sa, ra, sd, rd, sg, rg,
):
    core = lax.axis_index("inner")
    chip = lax.axis_index("outer")
    me = 2 * chip + core
    mine = lax.div(me, 4)
    dp = lax.axis_index("dp")
    chips = n // 2
    sibling = {"inner": 1 - core}
    barrier = pltpu.get_barrier_semaphore()

    def tell(i, c):
        pl.semaphore_signal(barrier, inc=1, device_id=device(lax.rem(me + i, n)), device_id_type=MESH)
        return c

    lax.fori_loop(1, n, tell, 0)
    for i in range(1, ways):
        pl.semaphore_signal(barrier, inc=1, device_id={"dp": lax.rem(dp + i, ways)}, device_id_type=MESH)
    pl.semaphore_wait(barrier, n + ways - 2)

    row, col, row_at, col_at = places()
    eye = row == col
    strict = col_at < row_at
    reads = read_mask(col)
    many = [(h, b) for h in range(GROUP) for b in range(2)]
    count = len(many)
    one = jnp.where(eye, 1.0, 0.0)
    steps = HEADS // GROUP

    def level(s):
        shift = s.bit_length() - 1
        rb, cb = row_at >> shift, col_at >> shift
        return ((rb >> 1) == (cb >> 1)) & ((rb & 1) == 1) & ((cb & 1) == 0)

    def masked(pair, mask):
        return tuple(jnp.where(mask, x.astype(F32), 0.0).astype(BF16) for x in pair)

    def send_maps(h):
        for e in range(2):
            d = 4 * h + 2 * e + core

            @pl.when(d != me)
            def _():
                to(t_dev.at[h], t_all.at[me], st.at[d], rt.at[me], device(d)).start()

        for j in range(4):
            d = 4 * h + j

            @pl.when(d != me)
            def _():
                to(o_dev.at[d], o_all.at[me], so.at[d], ro.at[me], device(d)).start()

    def maps(step, c):
        heads = [step * GROUP + h for h in range(GROUP)]
        keys, vals, query, queries, ratecol, raterow = [], [], [], [], [], []
        for h, b in many:
            kr = two_keys(k, b, heads[h]).astype(F32)
            inv = inv_norm(kr)
            kinv[heads[h], b] = inv
            keys.append(split(kr * inv))
            put(knp, (heads[h], b), keys[-1])
            vals.append(two_keys(v, b, heads[h]))
            qr = q[tokens(b), columns(heads[h])].astype(F32)
            inv = inv_norm(qr)
            qinv[heads[h], b] = inv
            query.append(qr * inv)
            queries.append(split(query[-1]))
            put(qnp, (heads[h], b), queries[-1])
            r = rate[heads[h], b : b + 1, :]
            raterow.append(r)
            ratecol.append(jnp.sum(jnp.where(eye, r, 0.0), axis=1, keepdims=True))
        both = [nt(stacked(keys[i], queries[i]), keys[i]) for i in range(count)]
        lower = [jnp.where(strict, ratecol[i] * both[i][:DIM], 0.0) for i in range(count)]
        scores = [split(jnp.where(reads, both[i][DIM:], 0.0)) for i in range(count)]
        first = level(1)
        inverse = [one - jnp.where(first, lower[i], 0.0) for i in range(count)]
        lower = [split(x) for x in lower]
        s = 2
        while s < DIM:
            mask = level(s)
            halves = [split(x) for x in inverse]
            inner = [split(nn(masked(lower[i], mask), halves[i])) for i in range(count)]
            inverse = [inverse[i] - nn(halves[i], inner[i]) for i in range(count)]
            s *= 2
        scaled = [split(inverse[i] * raterow[i]) for i in range(count)]
        zero = jnp.zeros((DIM, DIM), BF16)
        pack = [beside(keys[i], (vals[i], zero)) for i in range(count)]
        solved = [nn(scaled[i], pack[i]) for i in range(count)]
        z = [split(nn(scores[i], scaled[i])) for i in range(count)]
        gmat = [split(tn(scaled[i], keys[i])) for i in range(count)]
        solved_p = [split(x) for x in solved]
        move = [tn(solved_p[i], keys[i]) for i in range(count)]
        trans = [one - move[i][:DIM] for i in range(count)]
        offs = [move[i][DIM:] for i in range(count)]
        trans_p = [split(x) for x in trans]
        offs_p = [split(x) for x in offs]
        for h in range(GROUP):
            a, b = 2 * h, 2 * h + 1
            through = nn(stacked(trans_p[a], offs_p[a]), trans_p[b])
            t_dev[heads[h]] = through[:DIM]
            o_now = through[DIM:] + offs[b]
            for j in range(4):
                o_dev[4 * heads[h] + j] = o_now[j * 32 : j * 32 + 32]
            send_maps(heads[h])
        zr = [nn(z[i], pack[i]) for i in range(count)]
        qe = [query[i] - zr[i][:, :DIM] for i in range(count)]
        y = [zr[i][:, DIM:] for i in range(count)]
        for i, (h, b) in enumerate(many):
            put(wp, (heads[h], b), tuple(x[:, :DIM] for x in solved_p[i]))
            u[heads[h], b] = solved[i][:, DIM:]
            put(gp, (heads[h], b), gmat[i])
            put(zp, (heads[h], b), z[i])
            put(tp, (heads[h], b), trans_p[i])
        for h in range(GROUP):
            a, b = 2 * h, 2 * h + 1
            later = split(qe[b])
            back = nt(later, stacked(trans_p[a], offs_p[a]))
            put(q_dev, (heads[h], slice(0, HALF)), split(qe[a]))
            put(q_dev, (heads[h], slice(HALF, DIM)), split(back[:, :DIM]))
            y_dev[heads[h], :HALF] = y[a]
            y_dev[heads[h], HALF:] = y[b] + back[:, DIM:]
            o_blk[heads[h]] = offs[a]
            put(qep, (heads[h],), later)
        return c

    lax.fori_loop(0, steps, maps, 0)

    t_all[me] = t_dev[mine]
    o_all[me] = o_dev[me]

    def hand_over(i, c):
        p = 2 * lax.rem(chip - i + chips, chips) + core

        @pl.when(p != me)
        def _():
            to(t_dev.at[0], t_all.at[p], st.at[p], rt.at[p], device(p)).wait_recv()

        to(t_all.at[p], t_all.at[p], sf.at[p], rf.at[p], sibling).start()
        return c

    lax.fori_loop(0, chips, hand_over, 0)

    def handed(i, c):
        p = 2 * lax.rem(chip - i + chips, chips) + 1 - core
        to(t_all.at[p], t_all.at[p], sf.at[p], rf.at[p], sibling).wait_recv()
        return c

    lax.fori_loop(0, chips, handed, 0)

    def offset_here(i, c):
        p = lax.rem(me - i + n, n)
        to(o_dev.at[0], o_all.at[p], so.at[p], ro.at[p], device(p)).wait_recv()
        return c

    lax.fori_loop(1, n, offset_here, 0)

    groups = n // RUN
    wide = 4

    def products(i, c):
        base = [(i * wide + g) * RUN for g in range(wide)]
        trans = [split(t_all[p]) for p in base]
        offs = [o_all[p] for p in base]
        for g in range(wide):
            put(runs, (base[g],), trans[g])
            local[base[g]] = offs[g]
        trans = [stacked(trans[g], split(offs[g])) for g in range(wide)]
        for j in range(1, RUN):
            new = [nn(trans[g], split(t_all[base[g] + j])) for g in range(wide)]
            for g in range(wide):
                offs[g] = new[g][DIM:] + o_all[base[g] + j]
                local[base[g] + j] = offs[g]
                trans[g] = split(jnp.concatenate([new[g][:DIM], offs[g]], axis=0))
                put(runs, (base[g] + j,), tuple(x[:DIM] for x in trans[g]))
        return c

    lax.fori_loop(0, groups // wide, products, 0)

    def tell_state(p, now):
        s_all[p] = now

        @pl.when(p != me)
        def _():
            to(s_all.at[p], state.at[me], ss.at[p], rs.at[me], device(p)).start()

    def walk(g, now):
        base = g * RUN
        tell_state(base, now)
        halves = split(now)
        new = [nn(halves, get(runs, base + j)) + local[base + j] for j in range(RUN)]
        for j in range(RUN - 1):
            tell_state(base + j + 1, new[j])
        return new[RUN - 1]

    lax.fori_loop(0, groups, walk, jnp.zeros((DIM // 4, DIM), F32))
    state[me] = s_all[me]

    def suffixes(i, c):
        base = [(i * wide + g) * RUN for g in range(wide)]
        last = [split(t_all[p + RUN - 1]) for p in base]
        for g in range(wide):
            put(runs, (base[g] + RUN - 2,), last[g])
        for j in range(RUN - 2, 0, -1):
            last = [split(nn(split(t_all[base[g] + j]), last[g])) for g in range(wide)]
            for g in range(wide):
                put(runs, (base[g] + j - 1,), last[g])
        return c

    lax.fori_loop(0, groups // wide, suffixes, 0)

    def whole(ref, h):
        return ref[pl.ds(4 * h, 4)].reshape(DIM, DIM)

    def middle(step, c):
        heads = [step * GROUP + h for h in range(GROUP)]
        for h in heads:
            for j in range(4):
                d = 4 * h + j

                @pl.when(d != me)
                def _():
                    to(s_all.at[d], state.at[d], ss.at[d], rs.at[d], device(d)).wait_recv()

        qd = [get(q_dev, h) for h in heads]
        outs = [nt(qd[i], split(whole(state, h))) + y_dev[h] for i, h in enumerate(heads)]
        for i, h in enumerate(heads):
            out = outs[i]
            cot = cotan[:, columns(h)].astype(F32)
            scale = lax.rsqrt(jnp.mean(out * out, axis=1, keepdims=True) + EPS_OUT)
            normed = out * scale
            scaled = cot * gain[h]
            grad = scale * (scaled - normed * jnp.mean(normed * scaled, axis=1, keepdims=True))
            halves = split(grad)
            put(dop, (h,), halves)
            src = tn(halves, qd[i])
            gains = jnp.broadcast_to(jnp.sum(cot * normed, axis=0, keepdims=True), (8, DIM))
            for j in range(4):
                d = 4 * h + j
                source[d, 0:32] = src[j * 32 : j * 32 + 32]
                source[d, 32:40] = gains

                @pl.when(d != me)
                def _():
                    to(source.at[d], got.at[me], sx.at[d], rx.at[me], device(d)).start()

        return c

    lax.fori_loop(0, steps, middle, 0)
    got[me] = source[me]

    def by_states(step, c):
        heads = [step * GROUP + h for h in range(GROUP)]
        states, do = [], []
        for h in heads:
            s0 = split(whole(state, h))
            s1 = split(nn(s0, get(tp, h, 0)) + o_blk[h])
            do0, do1 = get(dop, h, slice(0, HALF)), get(dop, h, slice(HALF, DIM))
            states += [s0, s1]
            do += [do0, do1]
            src1[h] = tn(do1, get(qep, h))
        update = [split(u[heads[h], b] - nt(get(wp, heads[h], b), states[i])) for i, (h, b) in enumerate(many)]
        d_scores = [split(jnp.where(reads, nt(do[i], update[i]), 0.0)) for i in range(count)]
        for i, (h, b) in enumerate(many):
            at = (heads[h], b)
            put(sp, at, states[i])
            put(upd, at, update[i])
            hold[at] = tn(get(zp, *at), do[i])
            qn = get(qnp, *at)
            part[at] = tn(d_scores[i], qn)
            grad = nn_sum((do[i], states[i]), (d_scores[i], get(knp, *at)))
            unit = joined(qn)
            grad = qinv[at] * (grad - unit * jnp.sum(unit * grad, axis=1, keepdims=True))
            gq_out[tokens(b), columns(heads[h])] = grad.astype(BF16)
        return c

    lax.fori_loop(0, steps, by_states, 0)

    def source_here(i, gains):
        p = n - 1 - i

        @pl.when(p != me)
        def _():
            to(source.at[0], got.at[p], sx.at[p], rx.at[p], device(p)).wait_recv()

        return gains + got[p, 32:40]

    gains = lax.fori_loop(0, n, source_here, jnp.zeros((8, DIM), F32))
    g_all[dp] = gains
    for i in range(1, ways):
        other = lax.rem(dp + i, ways)
        to(g_all.at[dp], g_all.at[dp], sd.at[other], rd.at[dp], {"dp": other}).start()

    def locals_back(i, c):
        base = [(i * wide + g) * RUN for g in range(wide)]
        now = [got[p + RUN - 1, 0:32] for p in base]
        for g in range(wide):
            local[base[g] + RUN - 1] = now[g]
        for j in range(RUN - 1, 0, -1):
            new = [nt(split(now[g]), split(t_all[base[g] + j - 1])) for g in range(wide)]
            now = [new[g] + got[base[g] + j - 1, 0:32] for g in range(wide)]
            for g in range(wide):
                local[base[g] + j - 1] = now[g]
        return c

    lax.fori_loop(0, groups // wide, locals_back, 0)

    def tell_adjoint(p, now):
        a_all[p] = now

        @pl.when(p != me)
        def _():
            to(a_all.at[p], adjoint.at[me], sa.at[p], ra.at[me], device(p)).start()

    def walk_back(i, now):
        base = (groups - 1 - i) * RUN
        tell_adjoint(base + RUN - 1, now)
        halves = split(now)
        new = [nt(halves, get(runs, base + j)) for j in range(RUN)]
        for j in range(RUN - 2, -1, -1):
            tell_adjoint(base + j, new[j] + local[base + j + 1])
        return new[RUN - 1] + local[base]

    lax.fori_loop(0, groups, walk_back, jnp.zeros((DIM // 4, DIM), F32))
    adjoint[me] = a_all[me]

    for i in range(1, ways):
        other = lax.rem(dp + i, ways)
        to(g_all.at[other], g_all.at[other], sd.at[other], rd.at[other], {"dp": other}).wait()

    @pl.when(lax.rem(me, 4) == 0)
    def _():
        summed = g_all[0]
        for i in range(1, ways):
            summed = summed + g_all[i]
        total[mine] = summed

        def give(i, c):
            d = lax.rem(me + i, n)
            to(total.at[mine], total.at[mine], sg.at[d], rg.at[mine], device(d)).start()
            return c

        lax.fori_loop(1, n, give, 0)

    def final(step, c):
        heads = [step * GROUP + h for h in range(GROUP)]
        for h in heads:
            for j in range(4):
                d = 4 * h + j

                @pl.when(d != me)
                def _():
                    to(a_all.at[d], adjoint.at[d], sa.at[d], ra.at[d], device(d)).wait_recv()

        adjoints = []
        for h in heads:
            a1 = split(whole(adjoint, h))
            adjoints += [split(nt(a1, get(tp, h, 1)) + src1[h]), a1]
        places_of = [(heads[h], b) for h, b in many]
        target = [hold[at] + nt(get(gp, *at), adjoints[i]) for i, at in enumerate(places_of)]
        less = [split(-x) for x in target]
        update = [get(upd, *at) for at in places_of]
        d_gram = [jnp.where(strict, nt(less[i], update[i]), 0.0) for i in range(count)]
        d_gram = [split(x + x.T) for x in d_gram]
        for i, (h, b) in enumerate(many):
            at = places_of[i]
            kn = get(knp, *at)
            grad = part[at] + nn_sum((less[i], get(sp, *at)), (d_gram[i], kn), (update[i], adjoints[i]))
            unit = joined(kn)
            grad = kinv[at] * (grad - unit * jnp.sum(unit * grad, axis=1, keepdims=True))
            for j in range(2):
                gk_out[tokens(b), columns(heads[h], j)] = grad[tokens(j)].astype(BF16)
                gv_out[tokens(b), columns(heads[h], j)] = target[i][tokens(j)].astype(BF16)
        return c

    lax.fori_loop(0, steps, final, 0)

    @pl.when(lax.rem(me, 4) == 0)
    def _():
        def gone(i, c):
            d = lax.rem(me + i, n)
            to(total.at[mine], total.at[mine], sg.at[d], rg.at[mine], device(d)).wait_send()
            return c

        lax.fori_loop(1, n, gone, 0)

    def finish(i, c):
        d = lax.rem(me + i, n)
        to(o_dev.at[0], o_all.at[d], so.at[d], ro.at[d], device(d)).wait_send()
        to(s_all.at[d], state.at[d], ss.at[d], rs.at[d], device(d)).wait_send()
        to(source.at[d], got.at[d], sx.at[d], rx.at[d], device(d)).wait_send()
        to(a_all.at[d], adjoint.at[d], sa.at[d], ra.at[d], device(d)).wait_send()
        return c

    lax.fori_loop(1, n, finish, 0)

    def finish_maps(i, c):
        d = 2 * lax.rem(chip + i, chips) + core

        @pl.when(d != me)
        def _():
            to(t_dev.at[0], t_all.at[d], st.at[d], rt.at[d], device(d)).wait_send()

        to(t_all.at[d], t_all.at[d], sf.at[d], rf.at[d], sibling).wait_send()
        return c

    lax.fori_loop(0, chips, finish_maps, 0)

    for h in range(HEADS):

        @pl.when(me != 4 * h)
        def _(h=h):
            to(total.at[h], total.at[h], sg.at[h], rg.at[h], device(4 * h)).wait_recv()


def shape(*dims, dtype=F32):
    return jax.ShapeDtypeStruct(dims, dtype)


def layer(q, k, v, rate, cotan, gain, n, ways):
    def full(*dims):
        return pltpu.VMEM(dims, F32)

    def pair(*dims):
        return pltpu.VMEM((2, *dims), BF16)

    def dma(size):
        return pltpu.SemaphoreType.DMA((size,))

    square = (HEADS, DIM, DIM)
    blocks = (HEADS, 2, DIM, DIM)
    thin = (HEADS, 2, HALF, DIM)
    quarter = (n, DIM // 4, DIM)
    scratch = [
        full(*square), full(*quarter), pair(*square), full(*square),
        pair(*blocks), pair(*thin), full(HEADS, 2, DIM, 1), full(HEADS, 2, HALF, 1),
        pair(*blocks), full(*blocks), pair(*blocks), pair(*thin), pair(*blocks), full(*square), pair(HEADS, HALF, DIM),
        full(n, DIM, DIM), full(*quarter), pair(n, DIM, DIM), full(*quarter), full(*quarter), full(*quarter),
        pair(*square), full(n, 40, DIM), full(n, 40, DIM), full(*quarter), full(*quarter), full(ways, 8, DIM),
        pair(*blocks), pair(*blocks), full(*blocks), full(*blocks), full(*square),
    ]
    sems = [dma(n)] * 12 + [dma(ways)] * 2 + [dma(n), dma(HEADS)]
    wide = HEADS * DIM
    return pl.pallas_call(
        functools.partial(layer_kernel, n, ways),
        in_specs=[VMEM] * 6,
        out_specs=[VMEM] * 4,
        out_shape=[
            shape(DIM, wide, dtype=BF16),
            shape(DIM, 2 * wide, dtype=BF16),
            shape(DIM, 2 * wide, dtype=BF16),
            shape(HEADS, 8, DIM),
        ],
        scratch_shapes=scratch + sems,
        compiler_params=pltpu.CompilerParams(collective_id=0, has_side_effects=True, vmem_limit_bytes=LIMIT),
    )(q, k, v, rate, cotan, gain)


def on_device(queries, keys, values, betas, grad_out, gain):
    n = lax.axis_size("outer") * lax.axis_size("inner")
    ways = lax.axis_size("dp")
    k = keys[0].reshape(DIM, 2 * HEADS * DIM)
    v = values[0].reshape(DIM, 2 * HEADS * DIM)
    rate = betas[0].reshape(HEADS, 2, 2, HALF).transpose(0, 2, 1, 3).reshape(HEADS, 2, DIM)
    gq, gk, gv, total = layer(queries[0], k, v, rate, grad_out[0], gain.reshape(HEADS, 1, DIM), n, ways)
    grad_k = gk.reshape(1, DIM, 2, HEADS * DIM)
    grad_v = gv.reshape(1, DIM, 2, HEADS * DIM)
    gain_grad = total[:, 0, :].reshape(HEADS * DIM) * (1.0 / math.sqrt(DIM * n * ways))
    return gq[None], grad_k, grad_v, gain_grad


def solution(mesh):
    seq = ("outer", "inner")
    return jax.shard_map(
        on_device,
        mesh=mesh,
        in_specs=(
            P("dp", seq, None),
            P("dp", seq, None, None),
            P("dp", seq, None, None),
            P("dp", None, None, seq),
            P("dp", seq, None),
            P(),
        ),
        out_specs=(P("dp", seq, None), P("dp", seq, None, None), P("dp", seq, None, None), P()),
        check_vma=False,
    )
```

time: 123 us -> 96.1 us (0.78)
  Pallas kernels: 115 us -> 88.5 us
    pallas_call x5 -> x1, Pallas kernels: 115 us -> 88.5 us  [layer(): pl.pallas_call(functools.partial(layer_kernel, n, ways), in_specs=[VMEM]...]
    reshape x0 -> x2, local copies, waits for them, and re-layouts: none -> 2.33 us  [the longest x1 1.17 us: on_device(): grad_k = gk.reshape(1, DIM, 2, HEADS * DIM)]
    unnamed x10 -> x13, local copies, waits for them, and re-layouts: 5.04 us -> 3.62 us
where the time goes in v2:
time: 96.1 us; the launch traced here: 96 us
  Pallas kernels  88.5 us (92%)
  local copies, waits for them, and re-layouts  6.14 us (6%)
    pallas_call x1, Pallas kernels, layer(): pl.pallas_call(functools.partial(layer_kernel, n, ways), in_specs=[VMEM]...  88.5 us
    unnamed x13, local copies, waits for them, and re-layouts  3.62 us

profile of v2, /device:TPU:1, one launch (start us, length us, event | category | flops | bytes accessed | tf_op | source)
XLA Modules:
  0.0 96.0 jit_solution(10553516540971969257)
XLA Ops:
  0.6 0.0 copy-start.4
  0.6 0.7 copy-done.4
  1.3 0.1 reshape_squeeze.12
  1.4 0.1 reshape.22.rate
  1.5 0.0 copy-start.3
  1.5 1.2 %copy.11 = bf16[16,8,2,1024]{3,1,2,0:T(8,128)(2,1)S(1)} copy(bf16[16,8,2,1024]{3,2,1,0:T(2,128)(2,1)} %bitcast.20) | data formatting | bytes 1048576
  2.7 0.0 copy-done.3
  2.8 0.0 copy-start
  2.8 0.0 copy-start.1
  2.8 0.0 copy-start.2
  2.8 0.1 copy.12
  2.9 0.8 copy-done
  3.7 0.1 copy-done.1
  3.8 0.0 copy-done.2
  3.8 88.5 %shard_map.93 = (bf16[128,1024]{1,0:T(8,128)(2,1)S(1)}, bf16[128,2048]{1,0:T(8,128)(2,1)S(1)}, bf16[128,2048]{1,0:T(8,128)(2,1)S(1)}, f32[8,8,128]{2,1,0:T(8,128)S(1)}) custom-call(bf16[128,1024]{1,0:T(8,128)(2,1)S(1)} %bitcast.17, bf16[128,2048]{1,0:T(8,128)(2,1)S(1)} %bitcast.14, bf16[128,2048]{1,0:T(8,128)(2,1)S(1)} %bitcast.15, ...), custom_call_target="tpu_custom_call" | custom-call | tf_op jit(solution)/shard_map/pallas_call | solution.py:576
  92.3 0.6 slice_multiply_fusion
  92.9 1.2 %reshape.24 = bf16[1,128,2,1024]{3,2,1,0:T(2,128)(2,1)} reshape(bf16[128,2048]{1,0:T(8,128)(2,1)S(1)} %get-tuple-element.9) | data formatting | bytes 1048576 | tf_op jit(solution)/shard_map/reshape | solution.py:598
  94.1 1.2 %reshape.25 = bf16[1,128,2,1024]{3,2,1,0:T(2,128)(2,1)} reshape(bf16[128,2048]{1,0:T(8,128)(2,1)S(1)} %get-tuple-element.10) | data formatting | bytes 1048576 | tf_op jit(solution)/shard_map/reshape | solution.py:599
  95.3 0.7 copy.16
  (1 shorter events, 0.0 us)
Async XLA Ops:
  0.6 0.7 copy-start.4
  1.5 1.2 %copy-start.3 = (bf16[1,128,2,1024]{3,2,1,0:T(2,128)(2,1)S(1)}, bf16[1,128,2,1024]{3,2,1,0:T(2,128)(2,1)}, u32[]{:S(2)}) copy-start(bf16[1,128,2,1024]{3,2,1,0:T(2,128)(2,1)} %param.8) | copy-start | bytes 1572868
  2.8 1.0 copy-start
  2.8 1.0 %copy-start.1 = (bf16[1,128,1024]{2,1,0:T(8,128)(2,1)S(1)}, bf16[1,128,1024]{2,1,0:T(8,128)(2,1)}, u32[]{:S(2)}) copy-start(bf16[1,128,1024]{2,1,0:T(8,128)(2,1)} %param.10) | copy-start | bytes 786436
  2.8 1.0 %copy-start.2 = (f32[1024]{0:T(1024)S(1)}, f32[1024]{0:T(1024)}, u32[]{:S(2)}) copy-start(f32[1024]{0:T(1024)} %param.11) | copy-start | bytes 12292

commit v3 on v2

--- a/solution.py
+++ b/solution.py
@@ -120,36 +120,37 @@
     )
 
 
-def device(d):
-    return {"outer": lax.div(d, 2), "inner": lax.rem(d, 2)}
-
-
 def layer_kernel(
     n, ways,
     q, k, v, rate, cotan, gain,
     gq_out, gk_out, gv_out, total,
-    t_dev, o_dev, q_dev, y_dev, knp, qnp, kinv, qinv, wp, u, gp, zp, tp, o_blk, qep,
-    t_all, o_all, runs, local, s_all, state, dop, source, got, a_all, adjoint, g_all,
+    m_dev, m_sib, q_dev, q_grp, y_dev, knp, qnp, kinv, qinv, wp, u, gp, zp, tp, o_blk, qep,
+    m_out, m_all, t_all, runs, local, s_all, state, dop, src_two, src_got, src_own, src_next, source, got, a_all, adjoint, g_all,
     sp, upd, part, hold, src1,
-    st, rt, sf, rf, so, ro, ss, rs, sx, rx, sa, ra, sd, rd, sg, rg,
+    sw, rw, st, rt, sf, rf, ss, rs, shs, rhs, sy, ry, so, ro, sx, rx, sa, ra, sha, rha, sd, rd, sg, rg,
 ):
     core = lax.axis_index("inner")
     chip = lax.axis_index("outer")
-    me = 2 * chip + core
-    mine = lax.div(me, 4)
+    chips = n // 2
+    mine = lax.div(chip, 2)
     dp = lax.axis_index("dp")
-    chips = n // 2
     sibling = {"inner": 1 - core}
+    steps = HEADS // GROUP
+    quarter = DIM // 4
+
+    def there(x):
+        return {"outer": x}
+
     barrier = pltpu.get_barrier_semaphore()
 
     def tell(i, c):
-        pl.semaphore_signal(barrier, inc=1, device_id=device(lax.rem(me + i, n)), device_id_type=MESH)
-        return c
-
-    lax.fori_loop(1, n, tell, 0)
+        pl.semaphore_signal(barrier, inc=1, device_id=there(lax.rem(chip + i, chips)), device_id_type=MESH)
+        return c
+
+    lax.fori_loop(1, chips, tell, 0)
+    pl.semaphore_signal(barrier, inc=1, device_id=sibling, device_id_type=MESH)
     for i in range(1, ways):
         pl.semaphore_signal(barrier, inc=1, device_id={"dp": lax.rem(dp + i, ways)}, device_id_type=MESH)
-    pl.semaphore_wait(barrier, n + ways - 2)
 
     row, col, row_at, col_at = places()
     eye = row == col
@@ -158,7 +159,6 @@
     many = [(h, b) for h in range(GROUP) for b in range(2)]
     count = len(many)
     one = jnp.where(eye, 1.0, 0.0)
-    steps = HEADS // GROUP
 
     def level(s):
         shift = s.bit_length() - 1
@@ -168,23 +168,47 @@
     def masked(pair, mask):
         return tuple(jnp.where(mask, x.astype(F32), 0.0).astype(BF16) for x in pair)
 
-    def send_maps(h):
-        for e in range(2):
-            d = 4 * h + 2 * e + core
-
-            @pl.when(d != me)
-            def _():
-                to(t_dev.at[h], t_all.at[me], st.at[d], rt.at[me], device(d)).start()
-
-        for j in range(4):
-            d = 4 * h + j
-
-            @pl.when(d != me)
-            def _():
-                to(o_dev.at[d], o_all.at[me], so.at[d], ro.at[me], device(d)).start()
+    def turn(step):
+        first = lax.rem(step + chip, steps) * GROUP
+        return [first + h for h in range(GROUP)]
+
+    def swap(h):
+        return to(m_dev.at[h], m_sib.at[h], sw.at[h], rw.at[h], sibling)
+
+    def chip_maps(step):
+        heads = turn(step)
+        half = pl.ds(pl.multiple_of(core * HALF, HALF), HALF)
+        lead = core == 0
+        for h in heads:
+            swap(h).wait_recv()
+        rows, later, offs = [], [], []
+        for h in heads:
+            begin = [jnp.where(lead, m_dev[h, j, half], m_sib[h, j, half]) for j in range(2)]
+            rows.append(split(jnp.concatenate(begin, axis=0)))
+            later.append(split(jnp.where(lead, m_sib[h, 0], m_dev[h, 0])))
+            offs.append(jnp.where(lead, m_sib[h, 1, half], m_dev[h, 1, half]))
+        made = [nn(rows[i], later[i]) for i in range(GROUP)]
+        for i, h in enumerate(heads):
+            off = made[i][HALF:] + offs[i]
+            for e in range(2):
+                x = 2 * h + e
+                m_out[x, :HALF] = made[i][:HALF]
+                m_out[x, HALF:] = off[e * quarter : (e + 1) * quarter]
+
+                @pl.when(x != chip)
+                def _():
+                    to(m_out.at[x], m_all.at[chip], st.at[x], rt.at[chip], there(x)).start()
+
+        @pl.when(core == 1)
+        def _():
+            before = [stacked(split(m_sib[h, 0]), split(m_sib[h, 1])) for h in heads]
+            back = [nt(get(q_dev, h), before[i]) for i, h in enumerate(heads)]
+            for i, h in enumerate(heads):
+                put(q_grp, (h,), split(back[i][:, :DIM]))
+                y_dev[h] = y_dev[h] + back[i][:, DIM:]
 
     def maps(step, c):
-        heads = [step * GROUP + h for h in range(GROUP)]
+        heads = turn(step)
         keys, vals, query, queries, ratecol, raterow = [], [], [], [], [], []
         for h, b in many:
             kr = two_keys(k, b, heads[h]).astype(F32)
@@ -227,14 +251,6 @@
         offs = [move[i][DIM:] for i in range(count)]
         trans_p = [split(x) for x in trans]
         offs_p = [split(x) for x in offs]
-        for h in range(GROUP):
-            a, b = 2 * h, 2 * h + 1
-            through = nn(stacked(trans_p[a], offs_p[a]), trans_p[b])
-            t_dev[heads[h]] = through[:DIM]
-            o_now = through[DIM:] + offs[b]
-            for j in range(4):
-                o_dev[4 * heads[h] + j] = o_now[j * 32 : j * 32 + 32]
-            send_maps(heads[h])
         zr = [nn(z[i], pack[i]) for i in range(count)]
         qe = [query[i] - zr[i][:, :DIM] for i in range(count)]
         y = [zr[i][:, DIM:] for i in range(count)]
@@ -246,75 +262,82 @@
             put(tp, (heads[h], b), trans_p[i])
         for h in range(GROUP):
             a, b = 2 * h, 2 * h + 1
+            through = nn(stacked(trans_p[a], offs_p[a]), trans_p[b])
+            m_dev[heads[h], 0] = through[:DIM]
+            m_dev[heads[h], 1] = through[DIM:] + offs[b]
             later = split(qe[b])
             back = nt(later, stacked(trans_p[a], offs_p[a]))
-            put(q_dev, (heads[h], slice(0, HALF)), split(qe[a]))
-            put(q_dev, (heads[h], slice(HALF, DIM)), split(back[:, :DIM]))
+            for ref in (q_dev, q_grp):
+                put(ref, (heads[h], slice(0, HALF)), split(qe[a]))
+                put(ref, (heads[h], slice(HALF, DIM)), split(back[:, :DIM]))
             y_dev[heads[h], :HALF] = y[a]
             y_dev[heads[h], HALF:] = y[b] + back[:, DIM:]
             o_blk[heads[h]] = offs[a]
             put(qep, (heads[h],), later)
+
+        @pl.when(step == 0)
+        def _():
+            pl.semaphore_wait(barrier, chips + ways - 1)
+
+        for h in heads:
+            swap(h).start()
+
+        @pl.when(step > 0)
+        def _():
+            chip_maps(step - 1)
+
         return c
 
     lax.fori_loop(0, steps, maps, 0)
-
-    t_all[me] = t_dev[mine]
-    o_all[me] = o_dev[me]
+    chip_maps(steps - 1)
+    m_all[chip] = m_out[chip]
 
     def hand_over(i, c):
-        p = 2 * lax.rem(chip - i + chips, chips) + core
-
-        @pl.when(p != me)
-        def _():
-            to(t_dev.at[0], t_all.at[p], st.at[p], rt.at[p], device(p)).wait_recv()
-
-        to(t_all.at[p], t_all.at[p], sf.at[p], rf.at[p], sibling).start()
+        p = lax.rem(chip - i + chips, chips)
+
+        @pl.when(p != chip)
+        def _():
+            to(m_out.at[0], m_all.at[p], st.at[p], rt.at[p], there(p)).wait_recv()
+
+        t_all[p, core] = m_all[p, :HALF]
+        to(t_all.at[p, core], t_all.at[p, core], sf.at[p], rf.at[p], sibling).start()
         return c
 
     lax.fori_loop(0, chips, hand_over, 0)
 
     def handed(i, c):
-        p = 2 * lax.rem(chip - i + chips, chips) + 1 - core
-        to(t_all.at[p], t_all.at[p], sf.at[p], rf.at[p], sibling).wait_recv()
+        p = lax.rem(chip - i + chips, chips)
+        to(t_all.at[p, core], t_all.at[p, 1 - core], sf.at[p], rf.at[p], sibling).wait_recv()
         return c
 
     lax.fori_loop(0, chips, handed, 0)
 
-    def offset_here(i, c):
-        p = lax.rem(me - i + n, n)
-        to(o_dev.at[0], o_all.at[p], so.at[p], ro.at[p], device(p)).wait_recv()
-        return c
-
-    lax.fori_loop(1, n, offset_here, 0)
-
-    groups = n // RUN
-    wide = 4
-
-    def products(i, c):
-        base = [(i * wide + g) * RUN for g in range(wide)]
-        trans = [split(t_all[p]) for p in base]
-        offs = [o_all[p] for p in base]
-        for g in range(wide):
-            put(runs, (base[g],), trans[g])
-            local[base[g]] = offs[g]
-        trans = [stacked(trans[g], split(offs[g])) for g in range(wide)]
-        for j in range(1, RUN):
-            new = [nn(trans[g], split(t_all[base[g] + j])) for g in range(wide)]
-            for g in range(wide):
-                offs[g] = new[g][DIM:] + o_all[base[g] + j]
-                local[base[g] + j] = offs[g]
-                trans[g] = split(jnp.concatenate([new[g][:DIM], offs[g]], axis=0))
-                put(runs, (base[g] + j,), tuple(x[:DIM] for x in trans[g]))
-        return c
-
-    lax.fori_loop(0, groups // wide, products, 0)
+    groups = chips // RUN
+    bases = [g * RUN for g in range(groups)]
+
+    def transit(p):
+        return split(t_all[p].reshape(DIM, DIM))
+
+    trans = [transit(p) for p in bases]
+    offs = [m_all[p, HALF:] for p in bases]
+    for g, p in enumerate(bases):
+        put(runs, (p,), trans[g])
+        local[p] = offs[g]
+    trans = [stacked(trans[g], split(offs[g])) for g in range(groups)]
+    for j in range(1, RUN):
+        new = [nn(trans[g], transit(p + j)) for g, p in enumerate(bases)]
+        for g, p in enumerate(bases):
+            offs[g] = new[g][DIM:] + m_all[p + j, HALF:]
+            local[p + j] = offs[g]
+            trans[g] = split(jnp.concatenate([new[g][:DIM], offs[g]], axis=0))
+            put(runs, (p + j,), tuple(x[:DIM] for x in trans[g]))
 
     def tell_state(p, now):
         s_all[p] = now
 
-        @pl.when(p != me)
-        def _():
-            to(s_all.at[p], state.at[me], ss.at[p], rs.at[me], device(p)).start()
+        @pl.when(p != chip)
+        def _():
+            to(s_all.at[p], state.at[core, chip], ss.at[p], rs.at[chip], there(p)).start()
 
     def walk(g, now):
         base = g * RUN
@@ -325,36 +348,52 @@
             tell_state(base + j + 1, new[j])
         return new[RUN - 1]
 
-    lax.fori_loop(0, groups, walk, jnp.zeros((DIM // 4, DIM), F32))
-    state[me] = s_all[me]
-
-    def suffixes(i, c):
-        base = [(i * wide + g) * RUN for g in range(wide)]
-        last = [split(t_all[p + RUN - 1]) for p in base]
-        for g in range(wide):
-            put(runs, (base[g] + RUN - 2,), last[g])
-        for j in range(RUN - 2, 0, -1):
-            last = [split(nn(split(t_all[base[g] + j]), last[g])) for g in range(wide)]
-            for g in range(wide):
-                put(runs, (base[g] + j - 1,), last[g])
-        return c
-
-    lax.fori_loop(0, groups // wide, suffixes, 0)
+    lax.fori_loop(0, groups, walk, jnp.zeros((quarter, DIM), F32))
+    state[core, chip] = s_all[chip]
+
+    last = [transit(p + RUN - 1) for p in bases]
+    for g, p in enumerate(bases):
+        put(runs, (p + RUN - 2,), last[g])
+    for j in range(RUN - 2, 0, -1):
+        last = [split(nn(transit(p + j), last[g])) for g, p in enumerate(bases)]
+        for g, p in enumerate(bases):
+            put(runs, (p + j - 1,), last[g])
+
+    def arrive(ref, sent, send, recv, hand_send, hand_recv):
+        def one_head(h, c):
+            for e in range(2):
+                x = 2 * h + e
+
+                @pl.when(x != chip)
+                def _():
+                    to(sent.at[x], ref.at[core, x], send.at[x], recv.at[x], there(x)).wait_recv()
+
+            at = pl.ds(2 * h, 2)
+            to(ref.at[core, at], ref.at[core, at], hand_send.at[h], hand_recv.at[h], sibling).start()
+            return c
+
+        lax.fori_loop(0, HEADS, one_head, 0)
+
+    def handed_head(ref, h, hand_send, hand_recv):
+        at = pl.ds(2 * h, 2)
+        return to(ref.at[core, at], ref.at[1 - core, at], hand_send.at[h], hand_recv.at[h], sibling)
 
     def whole(ref, h):
-        return ref[pl.ds(4 * h, 4)].reshape(DIM, DIM)
+        return jnp.concatenate([ref[c, pl.ds(2 * h, 2)].reshape(HALF, DIM) for c in range(2)], axis=0)
+
+    arrive(state, s_all, ss, rs, shs, rhs)
+
+    def swap_source(h):
+        return to(src_two.at[h, 1 - core], src_got.at[h], sy.at[h], ry.at[h], sibling)
+
+    def next_source(h):
+        return to(src_own.at[h], src_next.at[h], so.at[h], ro.at[h], sibling)
 
     def middle(step, c):
         heads = [step * GROUP + h for h in range(GROUP)]
         for h in heads:
-            for j in range(4):
-                d = 4 * h + j
-
-                @pl.when(d != me)
-                def _():
-                    to(s_all.at[d], state.at[d], ss.at[d], rs.at[d], device(d)).wait_recv()
-
-        qd = [get(q_dev, h) for h in heads]
+            handed_head(state, h, shs, rhs).wait_recv()
+        qd = [get(q_grp, h) for h in heads]
         outs = [nt(qd[i], split(whole(state, h))) + y_dev[h] for i, h in enumerate(heads)]
         for i, h in enumerate(heads):
             out = outs[i]
@@ -367,25 +406,48 @@
             put(dop, (h,), halves)
             src = tn(halves, qd[i])
             gains = jnp.broadcast_to(jnp.sum(cot * normed, axis=0, keepdims=True), (8, DIM))
-            for j in range(4):
-                d = 4 * h + j
-                source[d, 0:32] = src[j * 32 : j * 32 + 32]
-                source[d, 32:40] = gains
-
-                @pl.when(d != me)
-                def _():
-                    to(source.at[d], got.at[me], sx.at[d], rx.at[me], device(d)).start()
-
+            for j in range(2):
+                src_two[h, j, :HALF] = src[j * HALF : (j + 1) * HALF]
+                src_two[h, j, HALF:] = gains
+            swap_source(h).start()
         return c
 
     lax.fori_loop(0, steps, middle, 0)
-    got[me] = source[me]
+
+    def chip_source(h, c):
+        swap_source(h).wait_recv()
+        both = src_two[h, core] + src_got[h]
+        for e in range(2):
+            x = 2 * h + e
+            source[x, :quarter] = both[e * quarter : (e + 1) * quarter]
+            source[x, quarter:] = both[HALF:]
+
+            @pl.when(x != chip)
+            def _():
+                to(source.at[x], got.at[chip], sx.at[x], rx.at[chip], there(x)).start()
+
+        return c
+
+    lax.fori_loop(0, HEADS, chip_source, 0)
+    got[chip] = source[chip]
+
+    @pl.when(core == 1)
+    def _():
+        def own(step, c):
+            for h in [step * GROUP + h for h in range(GROUP)]:
+                src_own[h] = tn(get(dop, h), get(q_dev, h))
+                next_source(h).start()
+            return c
+
+        lax.fori_loop(0, steps, own, 0)
 
     def by_states(step, c):
         heads = [step * GROUP + h for h in range(GROUP)]
         states, do = [], []
         for h in heads:
-            s0 = split(whole(state, h))
+            begin = whole(state, h)
+            moved = nn(split(begin), split(m_sib[h, 0])) + m_sib[h, 1]
+            s0 = split(jnp.where(core == 0, begin, moved))
             s1 = split(nn(s0, get(tp, h, 0)) + o_blk[h])
             do0, do1 = get(dop, h, slice(0, HALF)), get(dop, h, slice(HALF, DIM))
             states += [s0, s1]
@@ -409,40 +471,35 @@
     lax.fori_loop(0, steps, by_states, 0)
 
     def source_here(i, gains):
-        p = n - 1 - i
-
-        @pl.when(p != me)
-        def _():
-            to(source.at[0], got.at[p], sx.at[p], rx.at[p], device(p)).wait_recv()
-
-        return gains + got[p, 32:40]
-
-    gains = lax.fori_loop(0, n, source_here, jnp.zeros((8, DIM), F32))
+        p = chips - 1 - i
+
+        @pl.when(p != chip)
+        def _():
+            to(source.at[0], got.at[p], sx.at[p], rx.at[p], there(p)).wait_recv()
+
+        return gains + got[p, quarter:]
+
+    gains = lax.fori_loop(0, chips, source_here, jnp.zeros((8, DIM), F32))
     g_all[dp] = gains
     for i in range(1, ways):
         other = lax.rem(dp + i, ways)
         to(g_all.at[dp], g_all.at[dp], sd.at[other], rd.at[dp], {"dp": other}).start()
 
-    def locals_back(i, c):
-        base = [(i * wide + g) * RUN for g in range(wide)]
-        now = [got[p + RUN - 1, 0:32] for p in base]
-        for g in range(wide):
-            local[base[g] + RUN - 1] = now[g]
-        for j in range(RUN - 1, 0, -1):
-            new = [nt(split(now[g]), split(t_all[base[g] + j - 1])) for g in range(wide)]
-            now = [new[g] + got[base[g] + j - 1, 0:32] for g in range(wide)]
-            for g in range(wide):
-                local[base[g] + j - 1] = now[g]
-        return c
-
-    lax.fori_loop(0, groups // wide, locals_back, 0)
+    now = [got[p + RUN - 1, :quarter] for p in bases]
+    for g, p in enumerate(bases):
+        local[p + RUN - 1] = now[g]
+    for j in range(RUN - 1, 0, -1):
+        new = [nt(split(now[g]), transit(p + j - 1)) for g, p in enumerate(bases)]
+        now = [new[g] + got[p + j - 1, :quarter] for g, p in enumerate(bases)]
+        for g, p in enumerate(bases):
+            local[p + j - 1] = now[g]
 
     def tell_adjoint(p, now):
         a_all[p] = now
 
-        @pl.when(p != me)
-        def _():
-            to(a_all.at[p], adjoint.at[me], sa.at[p], ra.at[me], device(p)).start()
+        @pl.when(p != chip)
+        def _():
+            to(a_all.at[p], adjoint.at[core, chip], sa.at[p], ra.at[chip], there(p)).start()
 
     def walk_back(i, now):
         base = (groups - 1 - i) * RUN
@@ -453,14 +510,14 @@
             tell_adjoint(base + j, new[j] + local[base + j + 1])
         return new[RUN - 1] + local[base]
 
-    lax.fori_loop(0, groups, walk_back, jnp.zeros((DIM // 4, DIM), F32))
-    adjoint[me] = a_all[me]
+    lax.fori_loop(0, groups, walk_back, jnp.zeros((quarter, DIM), F32))
+    adjoint[core, chip] = a_all[chip]
 
     for i in range(1, ways):
         other = lax.rem(dp + i, ways)
         to(g_all.at[other], g_all.at[other], sd.at[other], rd.at[other], {"dp": other}).wait()
 
-    @pl.when(lax.rem(me, 4) == 0)
+    @pl.when(lax.rem(chip, 2) == 0)
     def _():
         summed = g_all[0]
         for i in range(1, ways):
@@ -468,25 +525,31 @@
         total[mine] = summed
 
         def give(i, c):
-            d = lax.rem(me + i, n)
-            to(total.at[mine], total.at[mine], sg.at[d], rg.at[mine], device(d)).start()
+            x = lax.rem(chip + i, chips)
+            to(total.at[mine], total.at[mine], sg.at[x], rg.at[mine], there(x)).start()
             return c
 
-        lax.fori_loop(1, n, give, 0)
+        lax.fori_loop(1, chips, give, 0)
+
+    @pl.when(core == 0)
+    def _():
+        def came(h, c):
+            next_source(h).wait_recv()
+            return c
+
+        lax.fori_loop(0, HEADS, came, 0)
+
+    arrive(adjoint, a_all, sa, ra, sha, rha)
 
     def final(step, c):
         heads = [step * GROUP + h for h in range(GROUP)]
         for h in heads:
-            for j in range(4):
-                d = 4 * h + j
-
-                @pl.when(d != me)
-                def _():
-                    to(a_all.at[d], adjoint.at[d], sa.at[d], ra.at[d], device(d)).wait_recv()
-
+            handed_head(adjoint, h, sha, rha).wait_recv()
         adjoints = []
         for h in heads:
-            a1 = split(whole(adjoint, h))
+            end = whole(adjoint, h)
+            moved = nt(split(end), split(m_sib[h, 0])) + src_next[h]
+            a1 = split(jnp.where(core == 0, moved, end))
             adjoints += [split(nt(a1, get(tp, h, 1)) + src1[h]), a1]
         places_of = [(heads[h], b) for h, b in many]
         target = [hold[at] + nt(get(gp, *at), adjoints[i]) for i, at in enumerate(places_of)]
@@ -507,42 +570,48 @@
 
     lax.fori_loop(0, steps, final, 0)
 
-    @pl.when(lax.rem(me, 4) == 0)
+    @pl.when(lax.rem(chip, 2) == 0)
     def _():
         def gone(i, c):
-            d = lax.rem(me + i, n)
-            to(total.at[mine], total.at[mine], sg.at[d], rg.at[mine], device(d)).wait_send()
+            x = lax.rem(chip + i, chips)
+            to(total.at[mine], total.at[mine], sg.at[x], rg.at[mine], there(x)).wait_send()
             return c
 
-        lax.fori_loop(1, n, gone, 0)
+        lax.fori_loop(1, chips, gone, 0)
 
     def finish(i, c):
-        d = lax.rem(me + i, n)
-        to(o_dev.at[0], o_all.at[d], so.at[d], ro.at[d], device(d)).wait_send()
-        to(s_all.at[d], state.at[d], ss.at[d], rs.at[d], device(d)).wait_send()
-        to(source.at[d], got.at[d], sx.at[d], rx.at[d], device(d)).wait_send()
-        to(a_all.at[d], adjoint.at[d], sa.at[d], ra.at[d], device(d)).wait_send()
-        return c
-
-    lax.fori_loop(1, n, finish, 0)
-
-    def finish_maps(i, c):
-        d = 2 * lax.rem(chip + i, chips) + core
-
-        @pl.when(d != me)
-        def _():
-            to(t_dev.at[0], t_all.at[d], st.at[d], rt.at[d], device(d)).wait_send()
-
-        to(t_all.at[d], t_all.at[d], sf.at[d], rf.at[d], sibling).wait_send()
-        return c
-
-    lax.fori_loop(0, chips, finish_maps, 0)
-
-    for h in range(HEADS):
-
-        @pl.when(me != 4 * h)
-        def _(h=h):
-            to(total.at[h], total.at[h], sg.at[h], rg.at[h], device(4 * h)).wait_recv()
+        x = lax.rem(chip + i, chips)
+        to(m_out.at[x], m_all.at[x], st.at[x], rt.at[x], there(x)).wait_send()
+        to(s_all.at[x], state.at[core, x], ss.at[x], rs.at[x], there(x)).wait_send()
+        to(source.at[x], got.at[x], sx.at[x], rx.at[x], there(x)).wait_send()
+        to(a_all.at[x], adjoint.at[core, x], sa.at[x], ra.at[x], there(x)).wait_send()
+        return c
+
+    lax.fori_loop(1, chips, finish, 0)
+
+    def finish_hand(p, c):
+        to(t_all.at[p, core], t_all.at[p, core], sf.at[p], rf.at[p], sibling).wait_send()
+        return c
+
+    lax.fori_loop(0, chips, finish_hand, 0)
+
+    def finish_heads(h, c):
+        swap(h).wait_send()
+        handed_head(state, h, shs, rhs).wait_send()
+        handed_head(adjoint, h, sha, rha).wait_send()
+        swap_source(h).wait_send()
+
+        @pl.when(core == 1)
+        def _():
+            next_source(h).wait_send()
+
+        @pl.when(2 * h != chip)
+        def _():
+            to(total.at[h], total.at[h], sg.at[h], rg.at[h], there(2 * h)).wait_recv()
+
+        return c
+
+    lax.fori_loop(0, HEADS, finish_heads, 0)
 
 
 def shape(*dims, dtype=F32):
@@ -559,19 +628,24 @@
     def dma(size):
         return pltpu.SemaphoreType.DMA((size,))
 
+    chips = n // 2
     square = (HEADS, DIM, DIM)
     blocks = (HEADS, 2, DIM, DIM)
     thin = (HEADS, 2, HALF, DIM)
-    quarter = (n, DIM // 4, DIM)
+    quarter = (chips, DIM // 4, DIM)
+    spread = (2, *quarter)
+    noted = (DIM // 4 + 8, DIM)
     scratch = [
-        full(*square), full(*quarter), pair(*square), full(*square),
+        full(*blocks), full(*blocks), pair(*square), pair(*square), full(*square),
         pair(*blocks), pair(*thin), full(HEADS, 2, DIM, 1), full(HEADS, 2, HALF, 1),
         pair(*blocks), full(*blocks), pair(*blocks), pair(*thin), pair(*blocks), full(*square), pair(HEADS, HALF, DIM),
-        full(n, DIM, DIM), full(*quarter), pair(n, DIM, DIM), full(*quarter), full(*quarter), full(*quarter),
-        pair(*square), full(n, 40, DIM), full(n, 40, DIM), full(*quarter), full(*quarter), full(ways, 8, DIM),
+        full(chips, 96, DIM), full(chips, 96, DIM), full(chips, 2, HALF, DIM), pair(chips, DIM, DIM), full(*quarter), full(*quarter),
+        full(*spread), pair(*square), full(HEADS, 2, HALF + 8, DIM), full(HEADS, HALF + 8, DIM), full(*square), full(*square),
+        full(chips, *noted), full(chips, *noted), full(*quarter), full(*spread), full(ways, 8, DIM),
         pair(*blocks), pair(*blocks), full(*blocks), full(*blocks), full(*square),
     ]
-    sems = [dma(n)] * 12 + [dma(ways)] * 2 + [dma(n), dma(HEADS)]
+    counts = [HEADS, chips, chips, chips, HEADS, HEADS, HEADS, chips, chips, HEADS, ways]
+    sems = [dma(size) for size in counts for _ in range(2)] + [dma(chips), dma(HEADS)]
     wide = HEADS * DIM
     return pl.pallas_call(
         functools.partial(layer_kernel, n, ways),

time: 96.1 us -> 70.5 us (0.73)
  Pallas kernels: 88.5 us -> 62.8 us
    pallas_call x1, Pallas kernels: 88.5 us -> 62.8 us  [layer(): pl.pallas_call(functools.partial(layer_kernel, n, ways), in_specs=[VMEM]...]
where the time goes in v3:
time: 70.5 us; the launch traced here: 70.3 us
  Pallas kernels  62.8 us (89%)
  local copies, waits for them, and re-layouts  6.14 us (9%)
    pallas_call x1, Pallas kernels, layer(): pl.pallas_call(functools.partial(layer_kernel, n, ways), in_specs=[VMEM]...  62.8 us
    unnamed x13, local copies, waits for them, and re-layouts  3.62 us

profile of v3, /device:TPU:1, one launch (start us, length us, event | category | flops | bytes accessed | tf_op | source)
XLA Modules:
  0.0 70.3 jit_solution(3897192863477684019)
XLA Ops:
  0.6 0.0 copy-start.4
  0.6 0.7 copy-done.4
  1.3 0.1 reshape_squeeze.12
  1.4 0.1 reshape.22.rate
  1.5 0.0 copy-start.3
  1.5 1.2 %copy.11 = bf16[16,8,2,1024]{3,1,2,0:T(8,128)(2,1)S(1)} copy(bf16[16,8,2,1024]{3,2,1,0:T(2,128)(2,1)} %bitcast.20) | data formatting | bytes 1048576
  2.7 0.0 copy-done.3
  2.8 0.0 copy-start
  2.8 0.0 copy-start.1
  2.8 0.0 copy-start.2
  2.8 0.1 copy.12
  2.9 0.8 %copy-done = bf16[1,128,1024]{2,1,0:T(8,128)(2,1)S(1)} copy-done((bf16[1,128,1024]{2,1,0:T(8,128)(2,1)S(1)}, bf16[1,128,1024]{2,1,0:T(8,128)(2,1)}, u32[]{:S(2)}) %copy-start) | copy-done | bytes 262168
  3.7 0.1 copy-done.1
  3.8 0.0 copy-done.2
  3.8 62.8 %shard_map.93 = (bf16[128,1024]{1,0:T(8,128)(2,1)S(1)}, bf16[128,2048]{1,0:T(8,128)(2,1)S(1)}, bf16[128,2048]{1,0:T(8,128)(2,1)S(1)}, f32[8,8,128]{2,1,0:T(8,128)S(1)}) custom-call(bf16[128,1024]{1,0:T(8,128)(2,1)S(1)} %bitcast.17, bf16[128,2048]{1,0:T(8,128)(2,1)S(1)} %bitcast.14, bf16[128,2048]{1,0:T(8,128)(2,1)S(1)} %bitcast.15, ...), custom_call_target="tpu_custom_call" | custom-call | tf_op jit(solution)/shard_map/pallas_call | solution.py:650
  66.6 0.6 slice_multiply_fusion
  67.2 1.2 %reshape.24 = bf16[1,128,2,1024]{3,2,1,0:T(2,128)(2,1)} reshape(bf16[128,2048]{1,0:T(8,128)(2,1)S(1)} %get-tuple-element.9) | data formatting | bytes 1048576 | tf_op jit(solution)/shard_map/reshape | solution.py:672
  68.4 1.2 %reshape.25 = bf16[1,128,2,1024]{3,2,1,0:T(2,128)(2,1)} reshape(bf16[128,2048]{1,0:T(8,128)(2,1)S(1)} %get-tuple-element.10) | data formatting | bytes 1048576 | tf_op jit(solution)/shard_map/reshape | solution.py:673
  69.6 0.7 copy.16
  (1 shorter events, 0.0 us)
Async XLA Ops:
  0.6 0.7 copy-start.4
  1.5 1.2 %copy-start.3 = (bf16[1,128,2,1024]{3,2,1,0:T(2,128)(2,1)S(1)}, bf16[1,128,2,1024]{3,2,1,0:T(2,128)(2,1)}, u32[]{:S(2)}) copy-start(bf16[1,128,2,1024]{3,2,1,0:T(2,128)(2,1)} %param.8) | copy-start | bytes 1572868
  2.8 1.0 %copy-start = (bf16[1,128,1024]{2,1,0:T(8,128)(2,1)S(1)}, bf16[1,128,1024]{2,1,0:T(8,128)(2,1)}, u32[]{:S(2)}) copy-start(bf16[1,128,1024]{2,1,0:T(8,128)(2,1)} %param.6) | copy-start | bytes 786436
  2.8 1.0 %copy-start.1 = (bf16[1,128,1024]{2,1,0:T(8,128)(2,1)S(1)}, bf16[1,128,1024]{2,1,0:T(8,128)(2,1)}, u32[]{:S(2)}) copy-start(bf16[1,128,1024]{2,1,0:T(8,128)(2,1)} %param.10) | copy-start | bytes 786436
  2.8 1.0 %copy-start.2 = (f32[1024]{0:T(1024)S(1)}, f32[1024]{0:T(1024)}, u32[]{:S(2)}) copy-start(f32[1024]{0:T(1024)} %param.11) | copy-start | bytes 12292

commit v4 on v3

--- a/solution.py
+++ b/solution.py
@@ -76,17 +76,12 @@
 
 def places():
     row = lax.broadcasted_iota(jnp.int32, (DIM, DIM), 0)
-    col = lax.broadcasted_iota(jnp.int32, (DIM, DIM), 1)
-
-    def order(n):
-        return jnp.where(n < HALF, 2 * n, 2 * n - (DIM - 1))
-
-    return row, col, order(row), order(col)
+    return row, lax.broadcasted_iota(jnp.int32, (DIM, DIM), 1)
 
 
 def read_mask(col):
     token = lax.broadcasted_iota(jnp.int32, (HALF, DIM), 0)
-    return jnp.where(col[:HALF] < HALF, col[:HALF], col[:HALF] - HALF) <= token
+    return (col[:HALF] >> 1) <= token
 
 
 def put(ref, at, pair):
@@ -102,8 +97,8 @@
     return pair[0].astype(F32) + pair[1].astype(F32)
 
 
-def columns(head, part=0):
-    return pl.ds(pl.multiple_of((part * HEADS + head) * DIM, DIM), DIM)
+def columns(head):
+    return pl.ds(pl.multiple_of(head * DIM, DIM), DIM)
 
 
 def tokens(block):
@@ -111,7 +106,7 @@
 
 
 def two_keys(ref, block, head):
-    return jnp.concatenate([ref[tokens(block), columns(head, j)] for j in range(2)], axis=0)
+    return ref[tokens(block), :, columns(head)].reshape(DIM, DIM)
 
 
 def to(src, dst, send, recv, target):
@@ -124,7 +119,7 @@
     n, ways,
     q, k, v, rate, cotan, gain,
     gq_out, gk_out, gv_out, total,
-    m_dev, m_sib, q_dev, q_grp, y_dev, knp, qnp, kinv, qinv, wp, u, gp, zp, tp, o_blk, qep,
+    m_dev, m_sib, q_dev, q_grp, y_dev, knp, qnp, kinv, qinv, wp, u, gp, zp, tp, o_blk, qep, xbp, scp,
     m_out, m_all, t_all, runs, local, s_all, state, dop, src_two, src_got, src_own, src_next, source, got, a_all, adjoint, g_all,
     sp, upd, part, hold, src1,
     sw, rw, st, rt, sf, rf, ss, rs, shs, rhs, sy, ry, so, ro, sx, rx, sa, ra, sha, rha, sd, rd, sg, rg,
@@ -152,9 +147,9 @@
     for i in range(1, ways):
         pl.semaphore_signal(barrier, inc=1, device_id={"dp": lax.rem(dp + i, ways)}, device_id_type=MESH)
 
-    row, col, row_at, col_at = places()
+    row, col = places()
     eye = row == col
-    strict = col_at < row_at
+    strict = col < row
     reads = read_mask(col)
     many = [(h, b) for h in range(GROUP) for b in range(2)]
     count = len(many)
@@ -162,7 +157,7 @@
 
     def level(s):
         shift = s.bit_length() - 1
-        rb, cb = row_at >> shift, col_at >> shift
+        rb, cb = row >> shift, col >> shift
         return ((rb >> 1) == (cb >> 1)) & ((rb & 1) == 1) & ((cb & 1) == 0)
 
     def masked(pair, mask):
@@ -199,6 +194,29 @@
                 def _():
                     to(m_out.at[x], m_all.at[chip], st.at[x], rt.at[chip], there(x)).start()
 
+    def query_side(step):
+        heads = [step * GROUP + h for h in range(GROUP)]
+        zero = jnp.zeros((DIM, DIM), BF16)
+        scaled = [get(xbp, heads[h], b) for h, b in many]
+        keys = [get(knp, heads[h], b) for h, b in many]
+        pack = [beside(keys[i], (two_keys(v, b, heads[h]), zero)) for i, (h, b) in enumerate(many)]
+        z = [split(nn(get(scp, heads[h], b), scaled[i])) for i, (h, b) in enumerate(many)]
+        zr = [nn(z[i], pack[i]) for i in range(count)]
+        qe = [joined(get(qnp, heads[h], b)) - zr[i][:, :DIM] for i, (h, b) in enumerate(many)]
+        for i, (h, b) in enumerate(many):
+            put(gp, (heads[h], b), split(tn(scaled[i], keys[i])))
+            put(zp, (heads[h], b), z[i])
+        for h in range(GROUP):
+            a, b = 2 * h, 2 * h + 1
+            later = split(qe[b])
+            back = nt(later, stacked(get(tp, heads[h], 0), split(o_blk[heads[h]])))
+            for ref in (q_dev, q_grp):
+                put(ref, (heads[h], slice(0, HALF)), split(qe[a]))
+                put(ref, (heads[h], slice(HALF, DIM)), split(back[:, :DIM]))
+            y_dev[heads[h], :HALF] = zr[a][:, DIM:]
+            y_dev[heads[h], HALF:] = zr[b][:, DIM:] + back[:, DIM:]
+            put(qep, (heads[h],), later)
+
         @pl.when(core == 1)
         def _():
             before = [stacked(split(m_sib[h, 0]), split(m_sib[h, 1])) for h in heads]
@@ -209,7 +227,7 @@
 
     def maps(step, c):
         heads = turn(step)
-        keys, vals, query, queries, ratecol, raterow = [], [], [], [], [], []
+        keys, vals, queries, ratecol, raterow = [], [], [], [], []
         for h, b in many:
             kr = two_keys(k, b, heads[h]).astype(F32)
             inv = inv_norm(kr)
@@ -220,8 +238,7 @@
             qr = q[tokens(b), columns(heads[h])].astype(F32)
             inv = inv_norm(qr)
             qinv[heads[h], b] = inv
-            query.append(qr * inv)
-            queries.append(split(query[-1]))
+            queries.append(split(qr * inv))
             put(qnp, (heads[h], b), queries[-1])
             r = rate[heads[h], b : b + 1, :]
             raterow.append(r)
@@ -243,37 +260,24 @@
         zero = jnp.zeros((DIM, DIM), BF16)
         pack = [beside(keys[i], (vals[i], zero)) for i in range(count)]
         solved = [nn(scaled[i], pack[i]) for i in range(count)]
-        z = [split(nn(scores[i], scaled[i])) for i in range(count)]
-        gmat = [split(tn(scaled[i], keys[i])) for i in range(count)]
         solved_p = [split(x) for x in solved]
         move = [tn(solved_p[i], keys[i]) for i in range(count)]
         trans = [one - move[i][:DIM] for i in range(count)]
         offs = [move[i][DIM:] for i in range(count)]
         trans_p = [split(x) for x in trans]
         offs_p = [split(x) for x in offs]
-        zr = [nn(z[i], pack[i]) for i in range(count)]
-        qe = [query[i] - zr[i][:, :DIM] for i in range(count)]
-        y = [zr[i][:, DIM:] for i in range(count)]
         for i, (h, b) in enumerate(many):
             put(wp, (heads[h], b), tuple(x[:, :DIM] for x in solved_p[i]))
             u[heads[h], b] = solved[i][:, DIM:]
-            put(gp, (heads[h], b), gmat[i])
-            put(zp, (heads[h], b), z[i])
+            put(xbp, (heads[h], b), scaled[i])
+            put(scp, (heads[h], b), scores[i])
             put(tp, (heads[h], b), trans_p[i])
         for h in range(GROUP):
             a, b = 2 * h, 2 * h + 1
             through = nn(stacked(trans_p[a], offs_p[a]), trans_p[b])
             m_dev[heads[h], 0] = through[:DIM]
             m_dev[heads[h], 1] = through[DIM:] + offs[b]
-            later = split(qe[b])
-            back = nt(later, stacked(trans_p[a], offs_p[a]))
-            for ref in (q_dev, q_grp):
-                put(ref, (heads[h], slice(0, HALF)), split(qe[a]))
-                put(ref, (heads[h], slice(HALF, DIM)), split(back[:, :DIM]))
-            y_dev[heads[h], :HALF] = y[a]
-            y_dev[heads[h], HALF:] = y[b] + back[:, DIM:]
             o_blk[heads[h]] = offs[a]
-            put(qep, (heads[h],), later)
 
         @pl.when(step == 0)
         def _():
@@ -292,6 +296,12 @@
     chip_maps(steps - 1)
     m_all[chip] = m_out[chip]
 
+    def deferred(step, c):
+        query_side(step)
+        return c
+
+    lax.fori_loop(0, steps // 2, deferred, 0)
+
     def hand_over(i, c):
         p = lax.rem(chip - i + chips, chips)
 
@@ -304,6 +314,7 @@
         return c
 
     lax.fori_loop(0, chips, hand_over, 0)
+    lax.fori_loop(steps // 2, steps, deferred, 0)
 
     def handed(i, c):
         p = lax.rem(chip - i + chips, chips)
@@ -388,6 +399,18 @@
 
     def next_source(h):
         return to(src_own.at[h], src_next.at[h], so.at[h], ro.at[h], sibling)
+
+    def chip_source(h):
+        swap_source(h).wait_recv()
+        both = src_two[h, core] + src_got[h]
+        for e in range(2):
+            x = 2 * h + e
+            source[x, :quarter] = both[e * quarter : (e + 1) * quarter]
+            source[x, quarter:] = both[HALF:]
+
+            @pl.when(x != chip)
+            def _():
+                to(source.at[x], got.at[chip], sx.at[x], rx.at[chip], there(x)).start()
 
     def middle(step, c):
         heads = [step * GROUP + h for h in range(GROUP)]
@@ -410,25 +433,18 @@
                 src_two[h, j, :HALF] = src[j * HALF : (j + 1) * HALF]
                 src_two[h, j, HALF:] = gains
             swap_source(h).start()
+
+        @pl.when(step > 0)
+        def _():
+            for h in heads:
+                chip_source(h - GROUP)
+
         return c
 
     lax.fori_loop(0, steps, middle, 0)
 
-    def chip_source(h, c):
-        swap_source(h).wait_recv()
-        both = src_two[h, core] + src_got[h]
-        for e in range(2):
-            x = 2 * h + e
-            source[x, :quarter] = both[e * quarter : (e + 1) * quarter]
-            source[x, quarter:] = both[HALF:]
-
-            @pl.when(x != chip)
-            def _():
-                to(source.at[x], got.at[chip], sx.at[x], rx.at[chip], there(x)).start()
-
-        return c
-
-    lax.fori_loop(0, HEADS, chip_source, 0)
+    for h in range(HEADS - GROUP, HEADS):
+        chip_source(h)
     got[chip] = source[chip]
 
     @pl.when(core == 1)
@@ -513,6 +529,16 @@
     lax.fori_loop(0, groups, walk_back, jnp.zeros((quarter, DIM), F32))
     adjoint[core, chip] = a_all[chip]
 
+    @pl.when(core == 0)
+    def _():
+        def came(h, c):
+            next_source(h).wait_recv()
+            return c
+
+        lax.fori_loop(0, HEADS, came, 0)
+
+    arrive(adjoint, a_all, sa, ra, sha, rha)
+
     for i in range(1, ways):
         other = lax.rem(dp + i, ways)
         to(g_all.at[other], g_all.at[other], sd.at[other], rd.at[other], {"dp": other}).wait()
@@ -530,16 +556,6 @@
             return c
 
         lax.fori_loop(1, chips, give, 0)
-
-    @pl.when(core == 0)
-    def _():
-        def came(h, c):
-            next_source(h).wait_recv()
-            return c
-
-        lax.fori_loop(0, HEADS, came, 0)
-
-    arrive(adjoint, a_all, sa, ra, sha, rha)
 
     def final(step, c):
         heads = [step * GROUP + h for h in range(GROUP)]
@@ -563,9 +579,8 @@
             grad = part[at] + nn_sum((less[i], get(sp, *at)), (d_gram[i], kn), (update[i], adjoints[i]))
             unit = joined(kn)
             grad = kinv[at] * (grad - unit * jnp.sum(unit * grad, axis=1, keepdims=True))
-            for j in range(2):
-                gk_out[tokens(b), columns(heads[h], j)] = grad[tokens(j)].astype(BF16)
-                gv_out[tokens(b), columns(heads[h], j)] = target[i][tokens(j)].astype(BF16)
+            gk_out[tokens(b), :, columns(heads[h])] = grad.astype(BF16).reshape(HALF, 2, DIM)
+            gv_out[tokens(b), :, columns(heads[h])] = target[i].astype(BF16).reshape(HALF, 2, DIM)
         return c
 
     lax.fori_loop(0, steps, final, 0)
@@ -639,6 +654,7 @@
         full(*blocks), full(*blocks), pair(*square), pair(*square), full(*square),
         pair(*blocks), pair(*thin), full(HEADS, 2, DIM, 1), full(HEADS, 2, HALF, 1),
         pair(*blocks), full(*blocks), pair(*blocks), pair(*thin), pair(*blocks), full(*square), pair(HEADS, HALF, DIM),
+        pair(*blocks), pair(*thin),
         full(chips, 96, DIM), full(chips, 96, DIM), full(chips, 2, HALF, DIM), pair(chips, DIM, DIM), full(*quarter), full(*quarter),
         full(*spread), pair(*square), full(HEADS, 2, HALF + 8, DIM), full(HEADS, HALF + 8, DIM), full(*square), full(*square),
         full(chips, *noted), full(chips, *noted), full(*quarter), full(*spread), full(ways, 8, DIM),
@@ -653,8 +669,8 @@
         out_specs=[VMEM] * 4,
         out_shape=[
             shape(DIM, wide, dtype=BF16),
-            shape(DIM, 2 * wide, dtype=BF16),
-            shape(DIM, 2 * wide, dtype=BF16),
+            shape(DIM, 2, wide, dtype=BF16),
+            shape(DIM, 2, wide, dtype=BF16),
             shape(HEADS, 8, DIM),
         ],
         scratch_shapes=scratch + sems,
@@ -665,14 +681,10 @@
 def on_device(queries, keys, values, betas, grad_out, gain):
     n = lax.axis_size("outer") * lax.axis_size("inner")
     ways = lax.axis_size("dp")
-    k = keys[0].reshape(DIM, 2 * HEADS * DIM)
-    v = values[0].reshape(DIM, 2 * HEADS * DIM)
-    rate = betas[0].reshape(HEADS, 2, 2, HALF).transpose(0, 2, 1, 3).reshape(HEADS, 2, DIM)
-    gq, gk, gv, total = layer(queries[0], k, v, rate, grad_out[0], gain.reshape(HEADS, 1, DIM), n, ways)
-    grad_k = gk.reshape(1, DIM, 2, HEADS * DIM)
-    grad_v = gv.reshape(1, DIM, 2, HEADS * DIM)
+    rate = betas[0].transpose(0, 2, 1).reshape(HEADS, 2, DIM)
+    gq, gk, gv, total = layer(queries[0], keys[0], values[0], rate, grad_out[0], gain.reshape(HEADS, 1, DIM), n, ways)
     gain_grad = total[:, 0, :].reshape(HEADS * DIM) * (1.0 / math.sqrt(DIM * n * ways))
-    return gq[None], grad_k, grad_v, gain_grad
+    return gq[None], gk[None], gv[None], gain_grad
 
 
 def solution(mesh):

time: 70.5 us -> 70.9 us (level)
  local copies, waits for them, and re-layouts: 6.14 us -> 6.85 us
    unnamed x13 -> x15, local copies, waits for them, and re-layouts: 3.62 us -> 6.64 us
    reshape x3 -> x1, local copies, waits for them, and re-layouts: 2.42 us -> 0.06 us  [on_device(): rate = betas[0].transpose(0, 2, 1).reshape(HEADS, 2, DIM)]
where the time goes in v4:
time: 70.9 us; the launch traced here: 70.6 us
  Pallas kernels  62.5 us (88%)
  local copies, waits for them, and re-layouts  6.85 us (10%)
    pallas_call x1, Pallas kernels, layer(): pl.pallas_call(functools.partial(layer_kernel, n, ways), in_specs=[VMEM]...  62.5 us
    unnamed x15, local copies, waits for them, and re-layouts  6.64 us

profile of v4, /device:TPU:1, one launch (start us, length us, event | category | flops | bytes accessed | tf_op | source)
XLA Modules:
  0.0 70.6 jit_solution(15205001725212865353)
XLA Ops:
  0.6 0.0 copy-start.5
  0.6 0.0 copy-start.2
  0.7 0.7 copy-done.5
  1.3 0.1 copy.11
  1.5 0.0 copy-start.4
  1.5 0.1 copy.12.rate
  1.6 0.0 copy-done.2
  1.6 0.6 copy-done.4
  2.2 0.0 copy-start
  2.2 1.0 %copy-done = bf16[1,128,2,1024]{3,2,1,0:T(2,128)(2,1)S(1)} copy-done((bf16[1,128,2,1024]{3,2,1,0:T(2,128)(2,1)S(1)}, bf16[1,128,2,1024]{3,2,1,0:T(2,128)(2,1)}, u32[]{:S(2)}) %copy-start) | copy-done | bytes 524312
  3.2 0.0 copy-start.1
  3.2 1.0 %copy-done.1 = bf16[1,128,2,1024]{3,2,1,0:T(2,128)(2,1)S(1)} copy-done((bf16[1,128,2,1024]{3,2,1,0:T(2,128)(2,1)S(1)}, bf16[1,128,2,1024]{3,2,1,0:T(2,128)(2,1)}, u32[]{:S(2)}) %copy-start.1) | copy-done | bytes 524312
  4.3 0.0 copy-start.3
  4.3 0.9 %copy-done.3 = bf16[1,128,1024]{2,1,0:T(8,128)(2,1)S(1)} copy-done((bf16[1,128,1024]{2,1,0:T(8,128)(2,1)S(1)}, bf16[1,128,1024]{2,1,0:T(8,128)(2,1)}, u32[]{:S(2)}) %copy-start.3) | copy-done | bytes 262168
  5.2 62.5 %shard_map.93 = (bf16[128,1024]{1,0:T(8,128)(2,1)S(1)}, bf16[128,2,1024]{2,1,0:T(2,128)(2,1)S(1)}, bf16[128,2,1024]{2,1,0:T(2,128)(2,1)S(1)}, f32[8,8,128]{2,1,0:T(8,128)S(1)}) custom-call(bf16[128,1024]{1,0:T(8,128)(2,1)S(1)} %bitcast.18, bf16[128,2,1024]{2,1,0:T(2,128)(2,1)S(1)} %bitcast.13, bf16[128,2,1024]{2,1,0:T(2,128)(2,1)S(1)} %bitcast.14, ...), custom_call_target="tpu_custom_call" | custom-call | tf_op jit(solution)/shard_map/pallas_call | solution.py:666
  67.7 0.6 slice_multiply_fusion
  68.3 0.7 copy.16
  69.0 0.8 %copy.17 = bf16[1,128,2,1024]{3,2,1,0:T(2,128)(2,1)} copy(bf16[1,128,2,1024]{3,2,1,0:T(2,128)(2,1)S(1)} %bitcast.16) | data formatting | bytes 1048576
  69.8 0.8 %copy.18 = bf16[1,128,2,1024]{3,2,1,0:T(2,128)(2,1)} copy(bf16[1,128,2,1024]{3,2,1,0:T(2,128)(2,1)S(1)} %bitcast.15) | data formatting | bytes 1048576
Async XLA Ops:
  0.6 0.7 copy-start.5
  0.6 1.0 %copy-start.2 = (bf16[1,128,1024]{2,1,0:T(8,128)(2,1)S(1)}, bf16[1,128,1024]{2,1,0:T(8,128)(2,1)}, u32[]{:S(2)}) copy-start(bf16[1,128,1024]{2,1,0:T(8,128)(2,1)} %param.6) | copy-start | bytes 786436
  1.5 0.7 %copy-start.4 = (f32[1024]{0:T(1024)S(1)}, f32[1024]{0:T(1024)}, u32[]{:S(2)}) copy-start(f32[1024]{0:T(1024)} %param.11) | copy-start | bytes 12292
  2.2 1.0 %copy-start = (bf16[1,128,2,1024]{3,2,1,0:T(2,128)(2,1)S(1)}, bf16[1,128,2,1024]{3,2,1,0:T(2,128)(2,1)}, u32[]{:S(2)}) copy-start(bf16[1,128,2,1024]{3,2,1,0:T(2,128)(2,1)} %param.7) | copy-start | bytes 1572868
  3.2 1.0 %copy-start.1 = (bf16[1,128,2,1024]{3,2,1,0:T(2,128)(2,1)S(1)}, bf16[1,128,2,1024]{3,2,1,0:T(2,128)(2,1)}, u32[]{:S(2)}) copy-start(bf16[1,128,2,1024]{3,2,1,0:T(2,128)(2,1)} %param.8) | copy-start | bytes 1572868
  4.3 0.9 %copy-start.3 = (bf16[1,128,1024]{2,1,0:T(8,128)(2,1)S(1)}, bf16[1,128,1024]{2,1,0:T(8,128)(2,1)}, u32[]{:S(2)}) copy-start(bf16[1,128,1024]{2,1,0:T(8,128)(2,1)} %param.10) | copy-start | bytes 786436

commit v5 on v4

--- a/solution.py
+++ b/solution.py
@@ -11,7 +11,7 @@
 HEADS = 8
 DIM = 128
 HALF = 64
-GROUP = 2
+GROUP = 4
 RUN = 4
 EPS_KEY = 1e-06
 EPS_OUT = 1e-05

time: 70.9 us -> 66.9 us (0.944)
  Pallas kernels: 62.5 us -> 58.5 us
    pallas_call x1, Pallas kernels: 62.5 us -> 58.5 us  [layer(): pl.pallas_call(functools.partial(layer_kernel, n, ways), in_specs=[VMEM]...]
where the time goes in v5:
time: 66.9 us; the launch traced here: 66.6 us
  Pallas kernels  58.5 us (87%)
  local copies, waits for them, and re-layouts  6.85 us (10%)
  between operations  0.68 us (1%)
    pallas_call x1, Pallas kernels, layer(): pl.pallas_call(functools.partial(layer_kernel, n, ways), in_specs=[VMEM]...  58.5 us
    unnamed x15, local copies, waits for them, and re-layouts  6.64 us

profile of v5, /device:TPU:1, one launch (start us, length us, event | category | flops | bytes accessed | tf_op | source)
XLA Modules:
  0.0 66.6 jit_solution(2826443098071318857)
XLA Ops:
  0.6 0.0 copy-start.5
  0.6 0.0 copy-start.2
  0.7 0.7 %copy-done.5 = f32[1,8,2,128]{3,2,1,0:T(2,128)S(1)} copy-done((f32[1,8,2,128]{3,2,1,0:T(2,128)S(1)}, f32[1,8,2,128]{3,2,1,0:T(2,128)}, u32[]{:S(2)}) %copy-start.5) | copy-done | bytes 8216
  1.3 0.1 copy.11
  1.5 0.0 copy-start.4
  1.5 0.1 copy.12.rate
  1.6 0.0 copy-done.2
  1.6 0.6 copy-done.4
  2.2 0.0 copy-start
  2.2 1.0 %copy-done = bf16[1,128,2,1024]{3,2,1,0:T(2,128)(2,1)S(1)} copy-done((bf16[1,128,2,1024]{3,2,1,0:T(2,128)(2,1)S(1)}, bf16[1,128,2,1024]{3,2,1,0:T(2,128)(2,1)}, u32[]{:S(2)}) %copy-start) | copy-done | bytes 524312
  3.2 0.0 copy-start.1
  3.2 1.0 %copy-done.1 = bf16[1,128,2,1024]{3,2,1,0:T(2,128)(2,1)S(1)} copy-done((bf16[1,128,2,1024]{3,2,1,0:T(2,128)(2,1)S(1)}, bf16[1,128,2,1024]{3,2,1,0:T(2,128)(2,1)}, u32[]{:S(2)}) %copy-start.1) | copy-done | bytes 524312
  4.3 0.0 copy-start.3
  4.3 0.9 %copy-done.3 = bf16[1,128,1024]{2,1,0:T(8,128)(2,1)S(1)} copy-done((bf16[1,128,1024]{2,1,0:T(8,128)(2,1)S(1)}, bf16[1,128,1024]{2,1,0:T(8,128)(2,1)}, u32[]{:S(2)}) %copy-start.3) | copy-done | bytes 262168
  5.2 58.5 %shard_map.93 = (bf16[128,1024]{1,0:T(8,128)(2,1)S(1)}, bf16[128,2,1024]{2,1,0:T(2,128)(2,1)S(1)}, bf16[128,2,1024]{2,1,0:T(2,128)(2,1)S(1)}, f32[8,8,128]{2,1,0:T(8,128)S(1)}) custom-call(bf16[128,1024]{1,0:T(8,128)(2,1)S(1)} %bitcast.18, bf16[128,2,1024]{2,1,0:T(2,128)(2,1)S(1)} %bitcast.13, bf16[128,2,1024]{2,1,0:T(2,128)(2,1)S(1)} %bitcast.14, ...), custom_call_target="tpu_custom_call" | custom-call | tf_op jit(solution)/shard_map/pallas_call | solution.py:666
  63.7 0.6 slice_multiply_fusion
  64.3 0.7 %copy.16 = bf16[1,128,1024]{2,1,0:T(8,128)(2,1)} copy(bf16[1,128,1024]{2,1,0:T(8,128)(2,1)S(1)} %bitcast.17) | data formatting | bytes 524288
  65.0 0.8 %copy.17 = bf16[1,128,2,1024]{3,2,1,0:T(2,128)(2,1)} copy(bf16[1,128,2,1024]{3,2,1,0:T(2,128)(2,1)S(1)} %bitcast.16) | data formatting | bytes 1048576
  65.8 0.8 %copy.18 = bf16[1,128,2,1024]{3,2,1,0:T(2,128)(2,1)} copy(bf16[1,128,2,1024]{3,2,1,0:T(2,128)(2,1)S(1)} %bitcast.15) | data formatting | bytes 1048576
Async XLA Ops:
  0.6 0.7 %copy-start.5 = (f32[1,8,2,128]{3,2,1,0:T(2,128)S(1)}, f32[1,8,2,128]{3,2,1,0:T(2,128)}, u32[]{:S(2)}) copy-start(f32[1,8,2,128]{3,2,1,0:T(2,128)} %param.9) | copy-start | bytes 24580
  0.6 1.0 %copy-start.2 = (bf16[1,128,1024]{2,1,0:T(8,128)(2,1)S(1)}, bf16[1,128,1024]{2,1,0:T(8,128)(2,1)}, u32[]{:S(2)}) copy-start(bf16[1,128,1024]{2,1,0:T(8,128)(2,1)} %param.6) | copy-start | bytes 786436
  1.5 0.7 %copy-start.4 = (f32[1024]{0:T(1024)S(1)}, f32[1024]{0:T(1024)}, u32[]{:S(2)}) copy-start(f32[1024]{0:T(1024)} %param.11) | copy-start | bytes 12292
  2.2 1.0 %copy-start = (bf16[1,128,2,1024]{3,2,1,0:T(2,128)(2,1)S(1)}, bf16[1,128,2,1024]{3,2,1,0:T(2,128)(2,1)}, u32[]{:S(2)}) copy-start(bf16[1,128,2,1024]{3,2,1,0:T(2,128)(2,1)} %param.7) | copy-start | bytes 1572868
  3.2 1.0 %copy-start.1 = (bf16[1,128,2,1024]{3,2,1,0:T(2,128)(2,1)S(1)}, bf16[1,128,2,1024]{3,2,1,0:T(2,128)(2,1)}, u32[]{:S(2)}) copy-start(bf16[1,128,2,1024]{3,2,1,0:T(2,128)(2,1)} %param.8) | copy-start | bytes 1572868
  4.3 0.9 %copy-start.3 = (bf16[1,128,1024]{2,1,0:T(8,128)(2,1)S(1)}, bf16[1,128,1024]{2,1,0:T(8,128)(2,1)}, u32[]{:S(2)}) copy-start(bf16[1,128,1024]{2,1,0:T(8,128)(2,1)} %param.10) | copy-start | bytes 786436

commit v6 on v5

--- a/solution.py
+++ b/solution.py
@@ -19,7 +19,8 @@
 BF16 = jnp.bfloat16
 MESH = pl.DeviceIdType.MESH
 VMEM = pl.BlockSpec(memory_space=pltpu.VMEM)
-LIMIT = 48 * 1024 * 1024
+FAR = pl.BlockSpec(memory_space=pltpu.HBM)
+LIMIT = 62 * 1024 * 1024
 
 
 def split(x):
@@ -117,12 +118,13 @@
 
 def layer_kernel(
     n, ways,
-    q, k, v, rate, cotan, gain,
-    gq_out, gk_out, gv_out, total,
+    q_far, k_far, v_far, rate, cotan_far, gain,
+    gq_far, gk_far, gv_far, total,
+    q, k, v, cotan, gq_out, gk_out, gv_out,
     m_dev, m_sib, q_dev, q_grp, y_dev, knp, qnp, kinv, qinv, wp, u, gp, zp, tp, o_blk, qep, xbp, scp,
     m_out, m_all, t_all, runs, local, s_all, state, dop, src_two, src_got, src_own, src_next, source, got, a_all, adjoint, g_all,
     sp, upd, part, hold, src1,
-    sw, rw, st, rt, sf, rf, ss, rs, shs, rhs, sy, ry, so, ro, sx, rx, sa, ra, sha, rha, sd, rd, sg, rg,
+    sw, rw, st, rt, sf, rf, ss, rs, shs, rhs, sy, ry, so, ro, sx, rx, sa, ra, sha, rha, sd, rd, sg, rg, fetched, stored,
 ):
     core = lax.axis_index("inner")
     chip = lax.axis_index("outer")
@@ -136,6 +138,10 @@
     def there(x):
         return {"outer": x}
 
+    far = ((k_far, k), (q_far, q), (v_far, v), (cotan_far, cotan))
+    fetch = [pltpu.make_async_copy(src, dst, fetched.at[i]) for i, (src, dst) in enumerate(far)]
+    for copy in fetch:
+        copy.start()
     barrier = pltpu.get_barrier_semaphore()
 
     def tell(i, c):
@@ -292,6 +298,8 @@
 
         return c
 
+    for copy in fetch[:3]:
+        copy.wait()
     lax.fori_loop(0, steps, maps, 0)
     chip_maps(steps - 1)
     m_all[chip] = m_out[chip]
@@ -441,6 +449,7 @@
 
         return c
 
+    fetch[3].wait()
     lax.fori_loop(0, steps, middle, 0)
 
     for h in range(HEADS - GROUP, HEADS):
@@ -485,6 +494,8 @@
         return c
 
     lax.fori_loop(0, steps, by_states, 0)
+    queries_out = pltpu.make_async_copy(gq_out, gq_far, stored.at[0])
+    queries_out.start()
 
     def source_here(i, gains):
         p = chips - 1 - i
@@ -556,6 +567,14 @@
             return c
 
         lax.fori_loop(1, chips, give, 0)
+
+    def stores(step):
+        cols = pl.ds(pl.multiple_of(step * GROUP * DIM, GROUP * DIM), GROUP * DIM)
+        pairs = ((gk_out, gk_far), (gv_out, gv_far))
+        return [
+            pltpu.make_async_copy(src.at[:, :, cols], dst.at[:, :, cols], stored.at[1 + 2 * step + i])
+            for i, (src, dst) in enumerate(pairs)
+        ]
 
     def final(step, c):
         heads = [step * GROUP + h for h in range(GROUP)]
@@ -581,9 +600,15 @@
             grad = kinv[at] * (grad - unit * jnp.sum(unit * grad, axis=1, keepdims=True))
             gk_out[tokens(b), :, columns(heads[h])] = grad.astype(BF16).reshape(HALF, 2, DIM)
             gv_out[tokens(b), :, columns(heads[h])] = target[i].astype(BF16).reshape(HALF, 2, DIM)
+        for copy in stores(step):
+            copy.start()
         return c
 
     lax.fori_loop(0, steps, final, 0)
+    queries_out.wait()
+    for step in range(steps):
+        for copy in stores(step):
+            copy.wait()
 
     @pl.when(lax.rem(chip, 2) == 0)
     def _():
@@ -650,7 +675,10 @@
     quarter = (chips, DIM // 4, DIM)
     spread = (2, *quarter)
     noted = (DIM // 4 + 8, DIM)
+    wide = HEADS * DIM
+    flat, deep = pltpu.VMEM((DIM, wide), BF16), pltpu.VMEM((DIM, 2, wide), BF16)
     scratch = [
+        flat, deep, deep, flat, flat, deep, deep,
         full(*blocks), full(*blocks), pair(*square), pair(*square), full(*square),
         pair(*blocks), pair(*thin), full(HEADS, 2, DIM, 1), full(HEADS, 2, HALF, 1),
         pair(*blocks), full(*blocks), pair(*blocks), pair(*thin), pair(*blocks), full(*square), pair(HEADS, HALF, DIM),
@@ -661,12 +689,11 @@
         pair(*blocks), pair(*blocks), full(*blocks), full(*blocks), full(*square),
     ]
     counts = [HEADS, chips, chips, chips, HEADS, HEADS, HEADS, chips, chips, HEADS, ways]
-    sems = [dma(size) for size in counts for _ in range(2)] + [dma(chips), dma(HEADS)]
-    wide = HEADS * DIM
+    sems = [dma(size) for size in counts for _ in range(2)] + [dma(chips), dma(HEADS), dma(4), dma(1 + 2 * HEADS // GROUP)]
     return pl.pallas_call(
         functools.partial(layer_kernel, n, ways),
-        in_specs=[VMEM] * 6,
-        out_specs=[VMEM] * 4,
+        in_specs=[FAR, FAR, FAR, VMEM, FAR, VMEM],
+        out_specs=[FAR, FAR, FAR, VMEM],
         out_shape=[
             shape(DIM, wide, dtype=BF16),
             shape(DIM, 2, wide, dtype=BF16),

time: 66.9 us -> 69.3 us (1.036)
  Pallas kernels: 58.5 us -> 61.7 us
  local copies, waits for them, and re-layouts: 6.85 us -> 5.2 us
  other arithmetic: 0.6 us -> 1.41 us
    pallas_call x1, Pallas kernels: 58.5 us -> 61.7 us  [layer(): pl.pallas_call(functools.partial(layer_kernel, n, ways), in_specs=[FAR, F...]
    unnamed x15 -> x9, local copies, waits for them, and re-layouts: 6.64 us -> 4.39 us
    mul x1, other arithmetic: 0.6 us -> 1.41 us  [on_device(): total[:, 0, :].reshape(HEADS * DIM) * (1.0 / math.sqrt(DIM * n * ways))]
where the time goes in v6:
time: 69.3 us; the launch traced here: 69 us
  Pallas kernels  61.7 us (89%)
  local copies, waits for them, and re-layouts  5.2 us (8%)
  other arithmetic  1.41 us (2%)
    pallas_call x1, Pallas kernels, layer(): pl.pallas_call(functools.partial(layer_kernel, n, ways), in_specs=[FAR, F...  61.7 us
    unnamed x9, local copies, waits for them, and re-layouts  4.39 us
    mul x1, other arithmetic, on_device(): total[:, 0, :].reshape(HEADS * DIM) * (1.0 / math.sqrt(DIM * n * ways))  1.41 us

profile of v6, /device:TPU:1, one launch (start us, length us, event | category | flops | bytes accessed | tf_op | source)
XLA Modules:
  0.0 69.0 jit_solution(2558733710753459432)
XLA Ops:
  0.6 0.0 copy-start.2
  0.6 0.7 copy-done.2
  1.3 0.1 copy.11
  1.5 0.7 copy.12.rate
  2.2 61.7 %shard_map.93 = (bf16[128,1024]{1,0:T(8,128)(2,1)}, bf16[128,2,1024]{2,1,0:T(2,128)(2,1)}, bf16[128,2,1024]{2,1,0:T(2,128)(2,1)}, f32[8,8,128]{2,1,0:T(8,128)}) custom-call(bf16[128,1024]{1,0:T(8,128)(2,1)} %bitcast.19, bf16[128,2,1024]{2,1,0:T(2,128)(2,1)} %bitcast.13, bf16[128,2,1024]{2,1,0:T(2,128)(2,1)} %bitcast.14, f32[8,2,128]{2,1,0:T(2,128)} %copy.12.rate, ...), custom_call_target="tpu_custom_call" | custom-call | tf_op jit(solution)/shard_map/pallas_call | solution.py:693
  63.9 0.0 copy-start.1
  63.9 1.4 %slice_multiply_fusion = f32[8,1,128]{2,1,0:T(1,128)} fusion(f32[8,8,128]{2,1,0:T(8,128)} %get-tuple-element.11), kind=kLoop, calls=%fused_computation | loop fusion | flops 1024 | bytes 8192 | tf_op jit(solution)/shard_map/mul | solution.py:713
  65.3 1.7 %copy.16 = bf16[1,128,1024]{2,1,0:T(8,128)(2,1)} copy(bf16[1,128,1024]{2,1,0:T(8,128)(2,1)} %bitcast.18) | data formatting | bytes 524288
  67.0 0.0 copy-done.1
  67.0 0.0 copy-start
  67.0 0.8 %copy.17 = bf16[1,128,2,1024]{3,2,1,0:T(2,128)(2,1)} copy(bf16[1,128,2,1024]{3,2,1,0:T(2,128)(2,1)S(1)} %bitcast.16) | data formatting | bytes 1048576
  67.8 0.4 copy-done
  68.2 0.8 %copy.18 = bf16[1,128,2,1024]{3,2,1,0:T(2,128)(2,1)} copy(bf16[1,128,2,1024]{3,2,1,0:T(2,128)(2,1)S(1)} %bitcast.15) | data formatting | bytes 1048576
Async XLA Ops:
  0.6 0.7 %copy-start.2 = (f32[1,8,2,128]{3,2,1,0:T(2,128)S(1)}, f32[1,8,2,128]{3,2,1,0:T(2,128)}, u32[]{:S(2)}) copy-start(f32[1,8,2,128]{3,2,1,0:T(2,128)} %param.9) | copy-start | bytes 24580
  63.9 3.1 %copy-start.1 = (bf16[128,2,1024]{2,1,0:T(2,128)(2,1)S(1)}, bf16[128,2,1024]{2,1,0:T(2,128)(2,1)}, u32[]{:S(2)}) copy-start(bf16[128,2,1024]{2,1,0:T(2,128)(2,1)} %get-tuple-element.9) | copy-start | bytes 1572868
  67.0 1.2 %copy-start = (bf16[128,2,1024]{2,1,0:T(2,128)(2,1)S(1)}, bf16[128,2,1024]{2,1,0:T(2,128)(2,1)}, u32[]{:S(2)}) copy-start(bf16[128,2,1024]{2,1,0:T(2,128)(2,1)} %get-tuple-element.10) | copy-start | bytes 1572868

commit v7 on v5

--- a/solution.py
+++ b/solution.py
@@ -113,6 +113,10 @@
     return pltpu.make_async_remote_copy(
         src_ref=src, dst_ref=dst, send_sem=send, recv_sem=recv, device_id=target, device_id_type=MESH
     )
+
+
+def home(h):
+    return 2 * h + lax.rem(lax.div(h, 2), 2)
 
 
 def layer_kernel(
@@ -128,10 +132,10 @@
     chip = lax.axis_index("outer")
     chips = n // 2
     mine = lax.div(chip, 2)
+    owner = home(mine) == chip
     dp = lax.axis_index("dp")
     sibling = {"inner": 1 - core}
     steps = HEADS // GROUP
-    quarter = DIM // 4
 
     def there(x):
         return {"outer": x}
@@ -184,15 +188,12 @@
             offs.append(jnp.where(lead, m_sib[h, 1, half], m_dev[h, 1, half]))
         made = [nn(rows[i], later[i]) for i in range(GROUP)]
         for i, h in enumerate(heads):
-            off = made[i][HALF:] + offs[i]
-            for e in range(2):
-                x = 2 * h + e
-                m_out[x, :HALF] = made[i][:HALF]
-                m_out[x, HALF:] = off[e * quarter : (e + 1) * quarter]
-
-                @pl.when(x != chip)
-                def _():
-                    to(m_out.at[x], m_all.at[chip], st.at[x], rt.at[chip], there(x)).start()
+            m_out[h, :HALF] = made[i][:HALF]
+            m_out[h, HALF:] = made[i][HALF:] + offs[i]
+
+            @pl.when(home(h) != chip)
+            def _():
+                to(m_out.at[h], m_all.at[chip], st.at[h], rt.at[chip], there(home(h))).start()
 
     def query_side(step):
         heads = [step * GROUP + h for h in range(GROUP)]
@@ -294,7 +295,7 @@
 
     lax.fori_loop(0, steps, maps, 0)
     chip_maps(steps - 1)
-    m_all[chip] = m_out[chip]
+    m_all[chip] = m_out[mine]
 
     def deferred(step, c):
         query_side(step)
@@ -307,13 +308,16 @@
 
         @pl.when(p != chip)
         def _():
-            to(m_out.at[0], m_all.at[p], st.at[p], rt.at[p], there(p)).wait_recv()
+            to(m_out.at[0], m_all.at[p], st.at[0], rt.at[p], there(p)).wait_recv()
 
         t_all[p, core] = m_all[p, :HALF]
         to(t_all.at[p, core], t_all.at[p, core], sf.at[p], rf.at[p], sibling).start()
         return c
 
-    lax.fori_loop(0, chips, hand_over, 0)
+    @pl.when(owner)
+    def _():
+        lax.fori_loop(0, chips, hand_over, 0)
+
     lax.fori_loop(steps // 2, steps, deferred, 0)
 
     def handed(i, c):
@@ -321,7 +325,6 @@
         to(t_all.at[p, core], t_all.at[p, 1 - core], sf.at[p], rf.at[p], sibling).wait_recv()
         return c
 
-    lax.fori_loop(0, chips, handed, 0)
 
     groups = chips // RUN
     bases = [g * RUN for g in range(groups)]
@@ -329,68 +332,66 @@
     def transit(p):
         return split(t_all[p].reshape(DIM, DIM))
 
-    trans = [transit(p) for p in bases]
-    offs = [m_all[p, HALF:] for p in bases]
-    for g, p in enumerate(bases):
-        put(runs, (p,), trans[g])
-        local[p] = offs[g]
-    trans = [stacked(trans[g], split(offs[g])) for g in range(groups)]
-    for j in range(1, RUN):
-        new = [nn(trans[g], transit(p + j)) for g, p in enumerate(bases)]
+    @pl.when(owner)
+    def _():
+        lax.fori_loop(0, chips, handed, 0)
+        trans = [transit(p) for p in bases]
+        offs = [m_all[p, HALF:] for p in bases]
         for g, p in enumerate(bases):
-            offs[g] = new[g][DIM:] + m_all[p + j, HALF:]
-            local[p + j] = offs[g]
-            trans[g] = split(jnp.concatenate([new[g][:DIM], offs[g]], axis=0))
-            put(runs, (p + j,), tuple(x[:DIM] for x in trans[g]))
-
-    def tell_state(p, now):
-        s_all[p] = now
-
-        @pl.when(p != chip)
-        def _():
-            to(s_all.at[p], state.at[core, chip], ss.at[p], rs.at[chip], there(p)).start()
-
-    def walk(g, now):
-        base = g * RUN
-        tell_state(base, now)
-        halves = split(now)
-        new = [nn(halves, get(runs, base + j)) + local[base + j] for j in range(RUN)]
-        for j in range(RUN - 1):
-            tell_state(base + j + 1, new[j])
-        return new[RUN - 1]
-
-    lax.fori_loop(0, groups, walk, jnp.zeros((quarter, DIM), F32))
-    state[core, chip] = s_all[chip]
-
-    last = [transit(p + RUN - 1) for p in bases]
-    for g, p in enumerate(bases):
-        put(runs, (p + RUN - 2,), last[g])
-    for j in range(RUN - 2, 0, -1):
-        last = [split(nn(transit(p + j), last[g])) for g, p in enumerate(bases)]
+            put(runs, (p,), trans[g])
+            local[p] = offs[g]
+        trans = [stacked(trans[g], split(offs[g])) for g in range(groups)]
+        for j in range(1, RUN):
+            new = [nn(trans[g], transit(p + j)) for g, p in enumerate(bases)]
+            for g, p in enumerate(bases):
+                offs[g] = new[g][DIM:] + m_all[p + j, HALF:]
+                local[p + j] = offs[g]
+                trans[g] = split(jnp.concatenate([new[g][:DIM], offs[g]], axis=0))
+                put(runs, (p + j,), tuple(x[:DIM] for x in trans[g]))
+
+        def tell_state(p, now):
+            s_all[p] = now
+
+            @pl.when(p != chip)
+            def _():
+                to(s_all.at[p], state.at[core, mine], ss.at[p], rs.at[mine], there(p)).start()
+
+        def walk(g, now):
+            base = g * RUN
+            tell_state(base, now)
+            halves = split(now)
+            new = [nn(halves, get(runs, base + j)) + local[base + j] for j in range(RUN)]
+            for j in range(RUN - 1):
+                tell_state(base + j + 1, new[j])
+            return new[RUN - 1]
+
+        lax.fori_loop(0, groups, walk, jnp.zeros((HALF, DIM), F32))
+        state[core, mine] = s_all[chip]
+
+        last = [transit(p + RUN - 1) for p in bases]
         for g, p in enumerate(bases):
-            put(runs, (p + j - 1,), last[g])
+            put(runs, (p + RUN - 2,), last[g])
+        for j in range(RUN - 2, 0, -1):
+            last = [split(nn(transit(p + j), last[g])) for g, p in enumerate(bases)]
+            for g, p in enumerate(bases):
+                put(runs, (p + j - 1,), last[g])
 
     def arrive(ref, sent, send, recv, hand_send, hand_recv):
         def one_head(h, c):
-            for e in range(2):
-                x = 2 * h + e
-
-                @pl.when(x != chip)
-                def _():
-                    to(sent.at[x], ref.at[core, x], send.at[x], recv.at[x], there(x)).wait_recv()
-
-            at = pl.ds(2 * h, 2)
-            to(ref.at[core, at], ref.at[core, at], hand_send.at[h], hand_recv.at[h], sibling).start()
+            @pl.when(home(h) != chip)
+            def _():
+                to(sent.at[0], ref.at[core, h], send.at[0], recv.at[h], there(home(h))).wait_recv()
+
+            to(ref.at[core, h], ref.at[core, h], hand_send.at[h], hand_recv.at[h], sibling).start()
             return c
 
         lax.fori_loop(0, HEADS, one_head, 0)
 
     def handed_head(ref, h, hand_send, hand_recv):
-        at = pl.ds(2 * h, 2)
-        return to(ref.at[core, at], ref.at[1 - core, at], hand_send.at[h], hand_recv.at[h], sibling)
+        return to(ref.at[core, h], ref.at[1 - core, h], hand_send.at[h], hand_recv.at[h], sibling)
 
     def whole(ref, h):
-        return jnp.concatenate([ref[c, pl.ds(2 * h, 2)].reshape(HALF, DIM) for c in range(2)], axis=0)
+        return jnp.concatenate([ref[c, h] for c in range(2)], axis=0)
 
     arrive(state, s_all, ss, rs, shs, rhs)
 
@@ -402,15 +403,11 @@
 
     def chip_source(h):
         swap_source(h).wait_recv()
-        both = src_two[h, core] + src_got[h]
-        for e in range(2):
-            x = 2 * h + e
-            source[x, :quarter] = both[e * quarter : (e + 1) * quarter]
-            source[x, quarter:] = both[HALF:]
-
-            @pl.when(x != chip)
-            def _():
-                to(source.at[x], got.at[chip], sx.at[x], rx.at[chip], there(x)).start()
+        source[h] = src_two[h, core] + src_got[h]
+
+        @pl.when(home(h) != chip)
+        def _():
+            to(source.at[h], got.at[chip], sx.at[h], rx.at[chip], there(home(h))).start()
 
     def middle(step, c):
         heads = [step * GROUP + h for h in range(GROUP)]
@@ -445,7 +442,7 @@
 
     for h in range(HEADS - GROUP, HEADS):
         chip_source(h)
-    got[chip] = source[chip]
+    got[chip] = source[mine]
 
     @pl.when(core == 1)
     def _():
@@ -486,48 +483,50 @@
 
     lax.fori_loop(0, steps, by_states, 0)
 
-    def source_here(i, gains):
-        p = chips - 1 - i
-
-        @pl.when(p != chip)
-        def _():
-            to(source.at[0], got.at[p], sx.at[p], rx.at[p], there(p)).wait_recv()
-
-        return gains + got[p, quarter:]
-
-    gains = lax.fori_loop(0, chips, source_here, jnp.zeros((8, DIM), F32))
-    g_all[dp] = gains
-    for i in range(1, ways):
-        other = lax.rem(dp + i, ways)
-        to(g_all.at[dp], g_all.at[dp], sd.at[other], rd.at[dp], {"dp": other}).start()
-
-    now = [got[p + RUN - 1, :quarter] for p in bases]
-    for g, p in enumerate(bases):
-        local[p + RUN - 1] = now[g]
-    for j in range(RUN - 1, 0, -1):
-        new = [nt(split(now[g]), transit(p + j - 1)) for g, p in enumerate(bases)]
-        now = [new[g] + got[p + j - 1, :quarter] for g, p in enumerate(bases)]
+    @pl.when(owner)
+    def _():
+        def source_here(i, gains):
+            p = chips - 1 - i
+
+            @pl.when(p != chip)
+            def _():
+                to(source.at[0], got.at[p], sx.at[0], rx.at[p], there(p)).wait_recv()
+
+            return gains + got[p, HALF:]
+
+        gains = lax.fori_loop(0, chips, source_here, jnp.zeros((8, DIM), F32))
+        g_all[dp] = gains
+        for i in range(1, ways):
+            other = lax.rem(dp + i, ways)
+            to(g_all.at[dp], g_all.at[dp], sd.at[other], rd.at[dp], {"dp": other}).start()
+
+        now = [got[p + RUN - 1, :HALF] for p in bases]
         for g, p in enumerate(bases):
-            local[p + j - 1] = now[g]
-
-    def tell_adjoint(p, now):
-        a_all[p] = now
-
-        @pl.when(p != chip)
-        def _():
-            to(a_all.at[p], adjoint.at[core, chip], sa.at[p], ra.at[chip], there(p)).start()
-
-    def walk_back(i, now):
-        base = (groups - 1 - i) * RUN
-        tell_adjoint(base + RUN - 1, now)
-        halves = split(now)
-        new = [nt(halves, get(runs, base + j)) for j in range(RUN)]
-        for j in range(RUN - 2, -1, -1):
-            tell_adjoint(base + j, new[j] + local[base + j + 1])
-        return new[RUN - 1] + local[base]
-
-    lax.fori_loop(0, groups, walk_back, jnp.zeros((quarter, DIM), F32))
-    adjoint[core, chip] = a_all[chip]
+            local[p + RUN - 1] = now[g]
+        for j in range(RUN - 1, 0, -1):
+            new = [nt(split(now[g]), transit(p + j - 1)) for g, p in enumerate(bases)]
+            now = [new[g] + got[p + j - 1, :HALF] for g, p in enumerate(bases)]
+            for g, p in enumerate(bases):
+                local[p + j - 1] = now[g]
+
+        def tell_adjoint(p, now):
+            a_all[p] = now
+
+            @pl.when(p != chip)
+            def _():
+                to(a_all.at[p], adjoint.at[core, mine], sa.at[p], ra.at[mine], there(p)).start()
+
+        def walk_back(i, now):
+            base = (groups - 1 - i) * RUN
+            tell_adjoint(base + RUN - 1, now)
+            halves = split(now)
+            new = [nt(halves, get(runs, base + j)) for j in range(RUN)]
+            for j in range(RUN - 2, -1, -1):
+                tell_adjoint(base + j, new[j] + local[base + j + 1])
+            return new[RUN - 1] + local[base]
+
+        lax.fori_loop(0, groups, walk_back, jnp.zeros((HALF, DIM), F32))
+        adjoint[core, mine] = a_all[chip]
 
     @pl.when(core == 0)
     def _():
@@ -539,12 +538,12 @@
 
     arrive(adjoint, a_all, sa, ra, sha, rha)
 
-    for i in range(1, ways):
-        other = lax.rem(dp + i, ways)
-        to(g_all.at[other], g_all.at[other], sd.at[other], rd.at[other], {"dp": other}).wait()
-
-    @pl.when(lax.rem(chip, 2) == 0)
+    @pl.when(owner)
     def _():
+        for i in range(1, ways):
+            other = lax.rem(dp + i, ways)
+            to(g_all.at[other], g_all.at[other], sd.at[other], rd.at[other], {"dp": other}).wait()
+
         summed = g_all[0]
         for i in range(1, ways):
             summed = summed + g_all[i]
@@ -585,30 +584,22 @@
 
     lax.fori_loop(0, steps, final, 0)
 
-    @pl.when(lax.rem(chip, 2) == 0)
+    @pl.when(owner)
     def _():
-        def gone(i, c):
+        def finish(i, c):
             x = lax.rem(chip + i, chips)
             to(total.at[mine], total.at[mine], sg.at[x], rg.at[mine], there(x)).wait_send()
+            to(s_all.at[x], state.at[core, mine], ss.at[x], rs.at[mine], there(x)).wait_send()
+            to(a_all.at[x], adjoint.at[core, mine], sa.at[x], ra.at[mine], there(x)).wait_send()
             return c
 
-        lax.fori_loop(1, chips, gone, 0)
-
-    def finish(i, c):
-        x = lax.rem(chip + i, chips)
-        to(m_out.at[x], m_all.at[x], st.at[x], rt.at[x], there(x)).wait_send()
-        to(s_all.at[x], state.at[core, x], ss.at[x], rs.at[x], there(x)).wait_send()
-        to(source.at[x], got.at[x], sx.at[x], rx.at[x], there(x)).wait_send()
-        to(a_all.at[x], adjoint.at[core, x], sa.at[x], ra.at[x], there(x)).wait_send()
-        return c
-
-    lax.fori_loop(1, chips, finish, 0)
-
-    def finish_hand(p, c):
-        to(t_all.at[p, core], t_all.at[p, core], sf.at[p], rf.at[p], sibling).wait_send()
-        return c
-
-    lax.fori_loop(0, chips, finish_hand, 0)
+        lax.fori_loop(1, chips, finish, 0)
+
+        def finish_hand(p, c):
+            to(t_all.at[p, core], t_all.at[p, core], sf.at[p], rf.at[p], sibling).wait_send()
+            return c
+
+        lax.fori_loop(0, chips, finish_hand, 0)
 
     def finish_heads(h, c):
         swap(h).wait_send()
@@ -620,9 +611,11 @@
         def _():
             next_source(h).wait_send()
 
-        @pl.when(2 * h != chip)
-        def _():
-            to(total.at[h], total.at[h], sg.at[h], rg.at[h], there(2 * h)).wait_recv()
+        @pl.when(home(h) != chip)
+        def _():
+            to(m_out.at[h], m_all.at[chip], st.at[h], rt.at[chip], there(home(h))).wait_send()
+            to(source.at[h], got.at[chip], sx.at[h], rx.at[chip], there(home(h))).wait_send()
+            to(total.at[h], total.at[h], sg.at[h], rg.at[h], there(home(h))).wait_recv()
 
         return c
 
@@ -647,17 +640,17 @@
     square = (HEADS, DIM, DIM)
     blocks = (HEADS, 2, DIM, DIM)
     thin = (HEADS, 2, HALF, DIM)
-    quarter = (chips, DIM // 4, DIM)
-    spread = (2, *quarter)
-    noted = (DIM // 4 + 8, DIM)
+    rows = (chips, HALF, DIM)
+    spread = (2, HEADS, HALF, DIM)
+    noted = (HALF + 8, DIM)
     scratch = [
         full(*blocks), full(*blocks), pair(*square), pair(*square), full(*square),
         pair(*blocks), pair(*thin), full(HEADS, 2, DIM, 1), full(HEADS, 2, HALF, 1),
         pair(*blocks), full(*blocks), pair(*blocks), pair(*thin), pair(*blocks), full(*square), pair(HEADS, HALF, DIM),
         pair(*blocks), pair(*thin),
-        full(chips, 96, DIM), full(chips, 96, DIM), full(chips, 2, HALF, DIM), pair(chips, DIM, DIM), full(*quarter), full(*quarter),
+        full(*square), full(chips, DIM, DIM), full(chips, 2, HALF, DIM), pair(chips, DIM, DIM), full(*rows), full(*rows),
         full(*spread), pair(*square), full(HEADS, 2, HALF + 8, DIM), full(HEADS, HALF + 8, DIM), full(*square), full(*square),
-        full(chips, *noted), full(chips, *noted), full(*quarter), full(*spread), full(ways, 8, DIM),
+        full(HEADS, *noted), full(chips, *noted), full(*rows), full(*spread), full(ways, 8, DIM),
         pair(*blocks), pair(*blocks), full(*blocks), full(*blocks), full(*square),
     ]
     counts = [HEADS, chips, chips, chips, HEADS, HEADS, HEADS, chips, chips, HEADS, ways]

time: 66.9 us -> 74 us (1.11)
  Pallas kernels: 58.5 us -> 65.6 us
    pallas_call x1, Pallas kernels: 58.5 us -> 65.6 us  [layer(): pl.pallas_call(functools.partial(layer_kernel, n, ways), in_specs=[VMEM]...]
where the time goes in v7:
time: 74 us; the launch traced here: 73.7 us
  Pallas kernels  65.6 us (89%)
  local copies, waits for them, and re-layouts  6.85 us (9%)
    pallas_call x1, Pallas kernels, layer(): pl.pallas_call(functools.partial(layer_kernel, n, ways), in_specs=[VMEM]...  65.6 us
    unnamed x15, local copies, waits for them, and re-layouts  6.64 us

profile of v7, /device:TPU:1, one launch (start us, length us, event | category | flops | bytes accessed | tf_op | source)
XLA Modules:
  0.0 73.7 jit_solution(11930407027264597207)
XLA Ops:
  0.6 0.0 copy-start.5
  0.6 0.0 copy-start.2
  0.7 0.7 copy-done.5
  1.3 0.1 copy.11
  1.5 0.0 copy-start.4
  1.5 0.1 copy.12.rate
  1.6 0.0 copy-done.2
  1.6 0.6 copy-done.4
  2.2 0.0 copy-start
  2.2 1.0 %copy-done = bf16[1,128,2,1024]{3,2,1,0:T(2,128)(2,1)S(1)} copy-done((bf16[1,128,2,1024]{3,2,1,0:T(2,128)(2,1)S(1)}, bf16[1,128,2,1024]{3,2,1,0:T(2,128)(2,1)}, u32[]{:S(2)}) %copy-start) | copy-done | bytes 524312
  3.2 0.0 copy-start.1
  3.2 1.0 %copy-done.1 = bf16[1,128,2,1024]{3,2,1,0:T(2,128)(2,1)S(1)} copy-done((bf16[1,128,2,1024]{3,2,1,0:T(2,128)(2,1)S(1)}, bf16[1,128,2,1024]{3,2,1,0:T(2,128)(2,1)}, u32[]{:S(2)}) %copy-start.1) | copy-done | bytes 524312
  4.3 0.0 copy-start.3
  4.3 0.9 %copy-done.3 = bf16[1,128,1024]{2,1,0:T(8,128)(2,1)S(1)} copy-done((bf16[1,128,1024]{2,1,0:T(8,128)(2,1)S(1)}, bf16[1,128,1024]{2,1,0:T(8,128)(2,1)}, u32[]{:S(2)}) %copy-start.3) | copy-done | bytes 262168
  5.2 65.6 %shard_map.93 = (bf16[128,1024]{1,0:T(8,128)(2,1)S(1)}, bf16[128,2,1024]{2,1,0:T(2,128)(2,1)S(1)}, bf16[128,2,1024]{2,1,0:T(2,128)(2,1)S(1)}, f32[8,8,128]{2,1,0:T(8,128)S(1)}) custom-call(bf16[128,1024]{1,0:T(8,128)(2,1)S(1)} %bitcast.18, bf16[128,2,1024]{2,1,0:T(2,128)(2,1)S(1)} %bitcast.13, bf16[128,2,1024]{2,1,0:T(2,128)(2,1)S(1)} %bitcast.14, ...), custom_call_target="tpu_custom_call" | custom-call | tf_op jit(solution)/shard_map/pallas_call | solution.py:659
  70.8 0.6 slice_multiply_fusion
  71.4 0.7 copy.16
  72.1 0.8 %copy.17 = bf16[1,128,2,1024]{3,2,1,0:T(2,128)(2,1)} copy(bf16[1,128,2,1024]{3,2,1,0:T(2,128)(2,1)S(1)} %bitcast.16) | data formatting | bytes 1048576
  72.9 0.8 %copy.18 = bf16[1,128,2,1024]{3,2,1,0:T(2,128)(2,1)} copy(bf16[1,128,2,1024]{3,2,1,0:T(2,128)(2,1)S(1)} %bitcast.15) | data formatting | bytes 1048576
Async XLA Ops:
  0.6 0.7 copy-start.5
  0.6 1.0 %copy-start.2 = (bf16[1,128,1024]{2,1,0:T(8,128)(2,1)S(1)}, bf16[1,128,1024]{2,1,0:T(8,128)(2,1)}, u32[]{:S(2)}) copy-start(bf16[1,128,1024]{2,1,0:T(8,128)(2,1)} %param.6) | copy-start | bytes 786436
  1.5 0.7 copy-start.4
  2.2 1.0 %copy-start = (bf16[1,128,2,1024]{3,2,1,0:T(2,128)(2,1)S(1)}, bf16[1,128,2,1024]{3,2,1,0:T(2,128)(2,1)}, u32[]{:S(2)}) copy-start(bf16[1,128,2,1024]{3,2,1,0:T(2,128)(2,1)} %param.7) | copy-start | bytes 1572868
  3.2 1.0 %copy-start.1 = (bf16[1,128,2,1024]{3,2,1,0:T(2,128)(2,1)S(1)}, bf16[1,128,2,1024]{3,2,1,0:T(2,128)(2,1)}, u32[]{:S(2)}) copy-start(bf16[1,128,2,1024]{3,2,1,0:T(2,128)(2,1)} %param.8) | copy-start | bytes 1572868
  4.3 0.9 %copy-start.3 = (bf16[1,128,1024]{2,1,0:T(8,128)(2,1)S(1)}, bf16[1,128,1024]{2,1,0:T(8,128)(2,1)}, u32[]{:S(2)}) copy-start(bf16[1,128,1024]{2,1,0:T(8,128)(2,1)} %param.10) | copy-start | bytes 786436

commit v8 on v5

--- a/solution.py
+++ b/solution.py
@@ -19,7 +19,8 @@
 BF16 = jnp.bfloat16
 MESH = pl.DeviceIdType.MESH
 VMEM = pl.BlockSpec(memory_space=pltpu.VMEM)
-LIMIT = 48 * 1024 * 1024
+FAR = pl.BlockSpec(memory_space=pltpu.HBM)
+LIMIT = 52 * 1024 * 1024
 
 
 def split(x):
@@ -117,12 +118,13 @@
 
 def layer_kernel(
     n, ways,
-    q, k, v, rate, cotan, gain,
+    q, k_far, v_far, rate, cotan, gain,
     gq_out, gk_out, gv_out, total,
+    k, v,
     m_dev, m_sib, q_dev, q_grp, y_dev, knp, qnp, kinv, qinv, wp, u, gp, zp, tp, o_blk, qep, xbp, scp,
     m_out, m_all, t_all, runs, local, s_all, state, dop, src_two, src_got, src_own, src_next, source, got, a_all, adjoint, g_all,
     sp, upd, part, hold, src1,
-    sw, rw, st, rt, sf, rf, ss, rs, shs, rhs, sy, ry, so, ro, sx, rx, sa, ra, sha, rha, sd, rd, sg, rg,
+    sw, rw, st, rt, sf, rf, ss, rs, shs, rhs, sy, ry, so, ro, sx, rx, sa, ra, sha, rha, sd, rd, sg, rg, fetched,
 ):
     core = lax.axis_index("inner")
     chip = lax.axis_index("outer")
@@ -136,6 +138,10 @@
     def there(x):
         return {"outer": x}
 
+    far = ((k_far, k), (v_far, v))
+    fetch = [pltpu.make_async_copy(src, dst, fetched.at[i]) for i, (src, dst) in enumerate(far)]
+    for copy in fetch:
+        copy.start()
     barrier = pltpu.get_barrier_semaphore()
 
     def tell(i, c):
@@ -292,6 +298,8 @@
 
         return c
 
+    for copy in fetch:
+        copy.wait()
     lax.fori_loop(0, steps, maps, 0)
     chip_maps(steps - 1)
     m_all[chip] = m_out[chip]
@@ -650,7 +658,10 @@
     quarter = (chips, DIM // 4, DIM)
     spread = (2, *quarter)
     noted = (DIM // 4 + 8, DIM)
+    wide = HEADS * DIM
+    deep = pltpu.VMEM((DIM, 2, wide), BF16)
     scratch = [
+        deep, deep,
         full(*blocks), full(*blocks), pair(*square), pair(*square), full(*square),
         pair(*blocks), pair(*thin), full(HEADS, 2, DIM, 1), full(HEADS, 2, HALF, 1),
         pair(*blocks), full(*blocks), pair(*blocks), pair(*thin), pair(*blocks), full(*square), pair(HEADS, HALF, DIM),
@@ -661,11 +672,10 @@
         pair(*blocks), pair(*blocks), full(*blocks), full(*blocks), full(*square),
     ]
     counts = [HEADS, chips, chips, chips, HEADS, HEADS, HEADS, chips, chips, HEADS, ways]
-    sems = [dma(size) for size in counts for _ in range(2)] + [dma(chips), dma(HEADS)]
-    wide = HEADS * DIM
+    sems = [dma(size) for size in counts for _ in range(2)] + [dma(chips), dma(HEADS), dma(2)]
     return pl.pallas_call(
         functools.partial(layer_kernel, n, ways),
-        in_specs=[VMEM] * 6,
+        in_specs=[VMEM, FAR, FAR, VMEM, VMEM, VMEM],
         out_specs=[VMEM] * 4,
         out_shape=[
             shape(DIM, wide, dtype=BF16),

time: 66.9 us -> 65.9 us (0.985)
  local copies, waits for them, and re-layouts: 6.85 us -> 4.77 us
  Pallas kernels: 58.5 us -> 59.7 us
    unnamed x15 -> x11, local copies, waits for them, and re-layouts: 6.64 us -> 4.56 us
    pallas_call x1, Pallas kernels: 58.5 us -> 59.7 us  [layer(): pl.pallas_call(functools.partial(layer_kernel, n, ways), in_specs=[VMEM,...]
where the time goes in v8:
time: 65.9 us; the launch traced here: 65.7 us
  Pallas kernels  59.7 us (91%)
  local copies, waits for them, and re-layouts  4.77 us (7%)
  between operations  0.67 us (1%)
    pallas_call x1, Pallas kernels, layer(): pl.pallas_call(functools.partial(layer_kernel, n, ways), in_specs=[VMEM,...  59.7 us
    unnamed x11, local copies, waits for them, and re-layouts  4.56 us

profile of v8, /device:TPU:1, one launch (start us, length us, event | category | flops | bytes accessed | tf_op | source)
XLA Modules:
  0.0 65.7 jit_solution(14644058214349363593)
XLA Ops:
  0.6 0.0 copy-start.3
  0.6 0.0 copy-start
  0.7 0.7 %copy-done.3 = f32[1,8,2,128]{3,2,1,0:T(2,128)S(1)} copy-done((f32[1,8,2,128]{3,2,1,0:T(2,128)S(1)}, f32[1,8,2,128]{3,2,1,0:T(2,128)}, u32[]{:S(2)}) %copy-start.3) | copy-done | bytes 8216
  1.3 0.1 copy.11
  1.5 0.0 copy-start.2
  1.5 0.1 copy.12.rate
  1.6 0.0 copy-done
  1.6 0.6 copy-done.2
  2.2 0.0 copy-start.1
  2.2 0.9 %copy-done.1 = bf16[1,128,1024]{2,1,0:T(8,128)(2,1)S(1)} copy-done((bf16[1,128,1024]{2,1,0:T(8,128)(2,1)S(1)}, bf16[1,128,1024]{2,1,0:T(8,128)(2,1)}, u32[]{:S(2)}) %copy-start.1) | copy-done | bytes 262168
  3.1 59.7 %shard_map.93 = (bf16[128,1024]{1,0:T(8,128)(2,1)S(1)}, bf16[128,2,1024]{2,1,0:T(2,128)(2,1)S(1)}, bf16[128,2,1024]{2,1,0:T(2,128)(2,1)S(1)}, f32[8,8,128]{2,1,0:T(8,128)S(1)}) custom-call(bf16[128,1024]{1,0:T(8,128)(2,1)S(1)} %bitcast.16, bf16[128,2,1024]{2,1,0:T(2,128)(2,1)} %bitcast.19, bf16[128,2,1024]{2,1,0:T(2,128)(2,1)} %bitcast.20, ...), custom_call_target="tpu_custom_call" | custom-call | tf_op jit(solution)/shard_map/pallas_call | solution.py:676
  62.8 0.6 slice_multiply_fusion
  63.4 0.7 %copy.16 = bf16[1,128,1024]{2,1,0:T(8,128)(2,1)} copy(bf16[1,128,1024]{2,1,0:T(8,128)(2,1)S(1)} %bitcast.15) | data formatting | bytes 524288
  64.1 0.8 %copy.17 = bf16[1,128,2,1024]{3,2,1,0:T(2,128)(2,1)} copy(bf16[1,128,2,1024]{3,2,1,0:T(2,128)(2,1)S(1)} %bitcast.14) | data formatting | bytes 1048576
  64.9 0.8 %copy.18 = bf16[1,128,2,1024]{3,2,1,0:T(2,128)(2,1)} copy(bf16[1,128,2,1024]{3,2,1,0:T(2,128)(2,1)S(1)} %bitcast.13) | data formatting | bytes 1048576
Async XLA Ops:
  0.6 0.7 %copy-start.3 = (f32[1,8,2,128]{3,2,1,0:T(2,128)S(1)}, f32[1,8,2,128]{3,2,1,0:T(2,128)}, u32[]{:S(2)}) copy-start(f32[1,8,2,128]{3,2,1,0:T(2,128)} %param.9) | copy-start | bytes 24580
  0.6 1.0 %copy-start = (bf16[1,128,1024]{2,1,0:T(8,128)(2,1)S(1)}, bf16[1,128,1024]{2,1,0:T(8,128)(2,1)}, u32[]{:S(2)}) copy-start(bf16[1,128,1024]{2,1,0:T(8,128)(2,1)} %param.6) | copy-start | bytes 786436
  1.5 0.7 %copy-start.2 = (f32[1024]{0:T(1024)S(1)}, f32[1024]{0:T(1024)}, u32[]{:S(2)}) copy-start(f32[1024]{0:T(1024)} %param.11) | copy-start | bytes 12292
  2.2 0.9 %copy-start.1 = (bf16[1,128,1024]{2,1,0:T(8,128)(2,1)S(1)}, bf16[1,128,1024]{2,1,0:T(8,128)(2,1)}, u32[]{:S(2)}) copy-start(bf16[1,128,1024]{2,1,0:T(8,128)(2,1)} %param.10) | copy-start | bytes 786436
